TPU v7x, 32 devices: a whole 2x2x4 slice. The times are simulated.
32 devices in a mesh: seq: 16 (over z, y, x), head: 2 (over core).
Axes of the slice: x: 2, y: 2, z: 4, core: 2. Of those that a mesh axis runs over, the one named last changes fastest.
Arguments:
- queries: bfloat16 [1, 2048, 2048], P(None, 'seq', 'head'), may hold values from -6 to 6
- keys: bfloat16 [1, 2048, 2048], P(None, 'seq', 'head'), may hold values from -8 to 8
- values: bfloat16 [1, 2048, 4096], P(None, 'seq', 'head'), may hold values from -12 to 12
- out_gate: bfloat16 [1, 2048, 4096], P(None, 'seq', 'head'), may hold values from -6 to 6
- log_decay: float32 [1, 32, 2048], P(None, 'head', 'seq'), may hold values from -0.7 to 0
- beta: float32 [1, 32, 2048], P(None, 'head', 'seq'), may hold values from 0 to 0.9
- norm_gain: float32 [128], replicated, may hold values from 0.5 to 1.5
- out_weight: bfloat16 [4096, 2048], P('head'), may hold values from -0.09375 to 0.09375
- owner: int32 [1, 32], P(None, 'head'), may hold values from 0 to 15, as said below
Outputs:
- layer_output: bfloat16 [2048, 1, 2048], P(('seq', 'head'))
- decode_states: float32 [16, 32, 128, 128], P('seq', 'head')
Inputs may be any that keep to these rules, and one draw needn't show every extreme that they name: For every value head h, owner[s, h] = (owner[0, h] + s * 16) modulo 16, so the prompts of one head have different owners.
All inputs are finite; a program needn't handle non-finite values.
Results may differ from a plain program's by a relative error of at most 0.006.
Values may be sent and summed in bfloat16 or wider, within the bound.
No kernel may reach another device: no remote copies, remote signals or barrier semaphores. Data moves between devices by JAX's collectives and lax.ppermute only.
A program may use at most 128 MiB of HBM per device.

v0:
```python
import jax
import jax.numpy as jnp
from jax import lax
from jax.sharding import PartitionSpec as P

DK = 128
DV = 128
BLOCK_TOKENS = 64


PRECISE = lax.Precision.HIGHEST


def prefix(value, axis, join, neutral):
    count, mine = (lax.axis_size(axis), lax.axis_index(axis))
    pieces = jax.tree.map(lambda part: lax.all_gather(part, axis), value)
    total = jax.tree.map(
        lambda part, zero: jnp.full_like(part, 0) + jnp.asarray(zero, part.dtype), value, neutral
    )

    def step(position, total):
        longer = join(total, jax.tree.map(lambda part: part[position], pieces))
        return jax.tree.map(lambda new, old: jnp.where(position < mine, new, old), longer, total)

    return lax.fori_loop(0, count - 1, step, total)


def from_root(value, axis, root):
    mine = lax.axis_index(axis) == root
    return lax.psum(jnp.where(mine, value, jnp.zeros_like(value)), axis)


def unit_rows(tensor, head_count, head_width):
    floats = tensor.astype(jnp.float32).reshape(
        tensor.shape[0], tensor.shape[1], head_count, head_width
    )
    return floats * lax.rsqrt(jnp.sum(floats * floats, axis=-1, keepdims=True) + 1e-06)


def to_spans(tensor, repeat):
    widened = jnp.repeat(tensor, repeat, axis=2)
    shaped = widened.reshape(
        widened.shape[0],
        widened.shape[1] // BLOCK_TOKENS,
        BLOCK_TOKENS,
        widened.shape[2],
        widened.shape[3],
    )
    return jnp.transpose(shaped, (1, 0, 3, 2, 4))


def gate_spans(tensor):
    shaped = tensor.reshape(
        tensor.shape[0], tensor.shape[1], tensor.shape[2] // BLOCK_TOKENS, BLOCK_TOKENS
    )
    return jnp.transpose(shaped, (2, 0, 1, 3))


def prepare(query_span, key_span, value_span, gate_span, beta_span):
    span_size = gate_span.shape[-1]
    cumulative = jnp.cumsum(gate_span, axis=-1)
    row_ids = lax.broadcasted_iota(jnp.int32, (span_size, span_size), 0)
    col_ids = lax.broadcasted_iota(jnp.int32, (span_size, span_size), 1)
    lower_mask = row_ids >= col_ids
    strict_mask = row_ids > col_ids
    log_gaps = jnp.where(lower_mask, cumulative[..., :, None] - cumulative[..., None, :], 0.0)
    decay_matrix = jnp.where(lower_mask, jnp.exp(log_gaps), 0.0)
    key_products = jnp.einsum("...td,...id->...ti", key_span, key_span, precision=PRECISE)
    system = jnp.where(strict_mask, beta_span[..., :, None] * decay_matrix * key_products, 0.0)
    system = system + jnp.eye(span_size, dtype=jnp.float32)
    scaled = jnp.exp(cumulative)[..., None]
    right_side = beta_span[..., None] * jnp.concatenate([value_span, scaled * key_span], axis=-1)
    solved = lax.linalg.triangular_solve(
        system, right_side, left_side=True, lower=True, unit_diagonal=True
    )
    update = solved[..., : value_span.shape[-1]]
    erasers = solved[..., value_span.shape[-1] :]
    mixing = decay_matrix * jnp.einsum(
        "...td,...id->...ti", query_span, key_span, precision=PRECISE
    )
    tail_keys = jnp.exp(cumulative[..., -1:] - cumulative)[..., None] * key_span
    return (cumulative, update, erasers, mixing, tail_keys)


def advance(state_now, cumulative, update, erasers, mixing, tail_keys, query_span):
    fresh_values = update - jnp.einsum("...ck,...kv->...cv", erasers, state_now, precision=PRECISE)
    output = jnp.exp(cumulative)[..., None] * jnp.einsum(
        "...ck,...kv->...cv", query_span, state_now, precision=PRECISE
    )
    output = output + jnp.einsum("...ti,...iv->...tv", mixing, fresh_values, precision=PRECISE)
    last_decay = jnp.exp(cumulative[..., -1])[..., None, None]
    state_after = last_decay * state_now + jnp.einsum(
        "...ck,...cv->...kv", tail_keys, fresh_values, precision=PRECISE
    )
    return (state_after, output)


def compose_maps(first_map, second_map):
    return jnp.einsum("...ij,...jk->...ik", first_map, second_map, precision=PRECISE)


def chain_forward(earlier_pair, later_pair):
    return (
        compose_maps(later_pair[0], earlier_pair[0]),
        compose_maps(later_pair[0], earlier_pair[1]) + later_pair[1],
    )


def local(queries, keys, values, out_gate, log_decay, beta, norm_gain, out_weight, owner):
    seq_count = queries.shape[0]
    tokens = queries.shape[1]
    value_heads = log_decay.shape[1]
    key_heads = queries.shape[2] // DK
    repeat = value_heads // key_heads
    query_all = to_spans(unit_rows(queries, key_heads, DK) * DK ** (-0.5), repeat)
    key_all = to_spans(unit_rows(keys, key_heads, DK), repeat)
    value_all = to_spans(values.astype(jnp.float32).reshape(seq_count, tokens, value_heads, DV), 1)
    cumulative, update, erasers, mixing, tail_keys = prepare(
        query_all, key_all, value_all, gate_spans(log_decay), gate_spans(beta)
    )
    identity = jnp.broadcast_to(jnp.eye(DK, dtype=jnp.float32), (seq_count, value_heads, DK, DK))
    zero_state = jnp.zeros((seq_count, value_heads, DK, DV), jnp.float32)
    span_moves = jnp.exp(cumulative[..., -1])[..., None, None] * jnp.eye(DK, dtype=jnp.float32)
    span_moves = span_moves - jnp.einsum(
        "...ck,...cj->...kj", tail_keys, erasers, precision=PRECISE
    )
    injects = jnp.einsum("...ck,...cv->...kv", tail_keys, update, precision=PRECISE)

    def compose_span(carried, pieces):
        move_now, add_now = carried
        move_span, inject_span = pieces
        return (
            (compose_maps(move_span, move_now), compose_maps(move_span, add_now) + inject_span),
            None,
        )

    (shard_move, shard_add), _ = lax.scan(
        compose_span, (identity, zero_state), (span_moves, injects)
    )
    entry_move, entry_state = prefix(
        (shard_move, shard_add), "seq", chain_forward, (identity, zero_state)
    )

    def run_span(state_now, pieces):
        cum_span, update_span, erase_span, mixing_span, tail_span, query_span = pieces
        return advance(
            state_now, cum_span, update_span, erase_span, mixing_span, tail_span, query_span
        )

    exit_state, outputs = lax.scan(
        run_span, entry_state, (cumulative, update, erasers, mixing, tail_keys, query_all)
    )
    final_state = from_root(
        exit_state.astype(jnp.bfloat16), "seq", lax.axis_size("seq") - 1
    ).astype(exit_state.dtype)
    my_index = lax.axis_index("seq")
    owned_mask = owner == my_index
    decode_states = jnp.sum(jnp.where(owned_mask[:, :, None, None], final_state, 0.0), axis=0)[None]
    readout = jnp.transpose(outputs, (0, 3, 1, 2, 4)).reshape(tokens, seq_count, value_heads, DV)
    gate_values = (
        jnp.transpose(out_gate, (1, 0, 2))
        .astype(jnp.float32)
        .reshape(tokens, seq_count, value_heads, DV)
    )
    normed = (
        readout
        * lax.rsqrt(jnp.mean(readout * readout, axis=-1, keepdims=True) + 1e-06)
        * norm_gain
        * jax.nn.silu(gate_values)
    )
    normed = normed.astype(jnp.bfloat16).reshape(tokens, seq_count, value_heads * DV)
    flattened = normed.reshape(
        lax.axis_size("head") * (tokens // lax.axis_size("head")) * seq_count, normed.shape[2]
    )
    partial_value = jnp.dot(flattened, out_weight, preferred_element_type=jnp.float32)
    layer_output = lax.psum_scatter(
        partial_value.reshape(
            lax.axis_size("head") * (tokens // lax.axis_size("head")),
            seq_count,
            out_weight.shape[1],
        ).astype(jnp.bfloat16),
        "head",
        scatter_dimension=0,
        tiled=True,
    )
    return (layer_output, decode_states)


def solution(mesh):
    placed = (
        P(None, "seq", "head"),
        P(None, "seq", "head"),
        P(None, "seq", "head"),
        P(None, "seq", "head"),
        P(None, "head", "seq"),
        P(None, "head", "seq"),
        P(),
        P("head", None),
        P(None, "head"),
    )
    return jax.shard_map(
        local,
        mesh=mesh,
        in_specs=placed,
        out_specs=(P(("seq", "head"), None, None), P("seq", "head", None, None)),
        check_vma=False,
    )
```

profile of v0, /device:TPU:0, one launch (start us, length us, event | category | flops | bytes accessed | tf_op | source)
XLA Modules:
  0.0 771.8 jit_solution(1550119193660975)
XLA Ops:
  11.9 2.9 fusion.50
  14.7 158.1 %custom-call.3 = f32[2,1,16,1,64,64]{4,5,3,2,1,0:T(8,128)S(1)} custom-call(f32[2,1,16,1,64,64]{5,4,3,2,1,0:T(8,128)} %fusion.50), custom_call_target="InvertDiagBlocksLowerTriangular" | custom-call | tf_op jit(solution)/shard_map/triangular_solve | solution.py:73
  176.6 4.8 convolution_bitcast_fusion.2
  181.4 3.7 subtract_bitcast_fusion
  186.4 10.7 %while.38 = (s32[]{:T(128)}, f32[1,16,128,128]{3,2,1,0:T(8,128)S(1)}, f32[1,16,128,128]{3,2,1,0:T(8,128)}, f32[2,1,16,128,128]{4,3,2,1,0:T(8,128)S(1)}, f32[2,1,16,128,128]{4,3,2,1,0:T(8,128)}, /*index=5*/s32[]{:T(128)}) while((s32[]{:T(128)}, f32[1,16,128,128]{3,2,1,0:T(8,128)S(1)}, f32[1,16,128,128]{3,2,1,0:T(8,128)}, ...), condition=%wide.region_3.4_spmd, body=%wide.region_2.0_spmd.sunk | while | flops 805568512 | bytes 19924068 | solution.py:137
  200.5 2.8 fusion.45
  204.9 187.5 %all-gather.5.cloned.1.call-done = f32[16,16,128,128]{3,2,1,0:T(8,128)} async-done(((f32[1,16,128,128]{3,2,1,0:T(8,128)}), f32[16,16,128,128]{3,2,1,0:T(8,128)}) %all-gather.5.cloned.1.call-update) | async-done | bytes 16777232 | tf_op jit(solution)/shard_map/all_gather | solution.py:16
  392.5 193.2 %all-gather.7.cloned.1.call-done = f32[16,16,128,128]{3,2,1,0:T(8,128)} async-done(((f32[1,16,128,128]{3,2,1,0:T(8,128)}), f32[16,16,128,128]{3,2,1,0:T(8,128)}) %all-gather.7.cloned.1.call-update) | async-done | bytes 16777232 | tf_op jit(solution)/shard_map/all_gather | solution.py:16
  585.7 44.1 %while.40 = (s32[]{:T(128)}, f32[1,16,128,128]{3,2,1,0:T(8,128)S(1)}, s32[]{:T(128)}, f32[16,1,16,128,128]{4,3,2,1,0:T(8,128)}, f32[16,1,16,128,128]{4,3,2,1,0:T(8,128)}, /*index=5*/s32[]{:T(128)}, s32[]{:T(128)}) while((s32[]{:T(128)}, f32[1,16,128,128]{3,2,1,0:T(8,128)S(1)}, s32[]{:T(128)}, f32[16,1,16,128,128]{4,3,2,1,0:T(8,128)}, ...), condition=%wide.region_5.6_spmd.clone, body=%wide.region_4.5_spmd.clone.sunk | while | flops 403701760 | bytes 7342687 | solution.py:25
  585.7 2.9 fusion.122
  588.8 2.8 fusion.122
  591.7 2.8 fusion.122
  594.6 2.8 fusion.122
  600.5 2.8 fusion.122
  606.3 2.8 fusion.122
  609.3 2.9 fusion.122
  612.2 2.8 fusion.122
  621.0 2.8 fusion.122
  624.0 2.8 fusion.122
  626.9 2.8 fusion.122
  629.8 14.7 %while.39 = (s32[]{:T(128)}, f32[1,16,128,128]{3,2,1,0:T(8,128)S(1)}, f32[2,1,16,64,128]{4,3,2,1,0:T(8,128)}, f32[2,1,16,64]{3,2,1,0:T(8,128)S(1)}, f32[2,1,16,6...) while((s32[]{:T(128)}, ...), condition=%wide.region_8.9_spmd, body=%wide.region_7.8_spmd.sunk | while | flops 705560576 | bytes 20470596 | solution.py:150
  649.3 6.2 fusion.39
  655.5 100.0 %all-reduce.2.cloned.1.call-done = bf16[1,16,128,128]{3,2,1,0:T(8,128)(2,1)} async-done(((bf16[1,16,128,128]{3,2,1,0:T(8,128)(2,1)}), bf16[1,16,128,128]{3,2,1,0:T(8,128)(2,1)}) %all-reduce.2.cloned.1.call-update) | async-done | bytes 524304 | tf_op jit(solution)/shard_map/psum | solution.py:30
  757.7 7.5 reduce-scatter.2.cloned.1.call-done
  (144 shorter events, 58.8 us)
Async XLA Ops:
  7.2 192.3 %copy-start = (f32[128]{0:T(128)S(1)}, f32[128]{0:T(128)}, u32[]{:S(2)}) copy-start(f32[128]{0:T(128)} %param.21) | copy-start | bytes 1540
  7.2 385.3 %all-gather.5.cloned.1.call-start = ((), (), s32[]{:S(2)}) async-start(), calls=%async_computation.3 | async-start | bytes 17825792 | tf_op jit(solution)/shard_map/all_gather | solution.py:16
  8.2 3.2 copy-start.15
  11.8 161.7 %copy-start.9 = (f32[128,8,2,128]{3,0,2,1:T(8,128)}, f32[128,8,2,128]{3,0,2,1:T(8,128)S(1)}, u32[]{:S(2)}) copy-start(f32[128,8,2,128]{3,0,2,1:T(8,128)S(1)} %broadcast_in_dim.73) | copy-start | bytes 3145732
  11.8 161.0 %copy-start.14 = (bf16[1,128,2048]{2,1,0:T(8,128)(2,1)S(1)}, bf16[1,128,2048]{2,1,0:T(8,128)(2,1)}, u32[]{:S(2)}) copy-start(bf16[1,128,2048]{2,1,0:T(8,128)(2,1)} %param.17) | copy-start | bytes 1572868
  174.1 7.3 copy-start.3
  176.6 4.9 copy-start.6
  186.4 1.9 copy-start.5
  191.7 1.9 copy-start.5
  197.0 1.8 copy-start.13
  198.0 387.7 %all-gather.7.cloned.1.call-start = ((), (), s32[]{:S(2)}) async-start(), calls=%async_computation.4 | async-start | bytes 17825792 | tf_op jit(solution)/shard_map/all_gather | solution.py:16
  198.8 556.8 %all-reduce.2.cloned.1.call-start = ((), (), s32[]{:S(2)}) async-start(), calls=%async_computation.2 | async-start | bytes 1048576 | tf_op jit(solution)/shard_map/psum | solution.py:30
  199.3 1.2 copy-start.10
  199.7 3.7 copy-start.7
  585.7 44.1 %copy-start.4 = (f32[2,1,16,64,128]{4,3,0,2,1:T(8,128)S(1)}, f32[2,1,16,64,128]{4,3,0,2,1:T(8,128)}, u32[]{:S(2)}) copy-start(f32[2,1,16,64,128]{4,3,0,2,1:T(8,128)} %copy-done.3) | copy-start | bytes 3145732
  629.8 2.5 copy-start.8
  629.8 3.2 copy-start.11
  634.1 1.0 copy-start.12
  637.1 2.5 copy-start.8
  637.2 3.2 copy-start.11
  648.0 1.3 copy-start.16
  648.9 116.3 %reduce-scatter.2.cloned.1.call-start = ((), (), s32[]{:S(2)}) async-start(), calls=%async_computation.1 | async-start | bytes 786432 | tf_op jit(solution)/shard_map/reduce_scatter | solution.py:176
  649.3 6.2 copy-start.17
  649.3 115.9 %copy-start.1 = (f32[128]{0:T(128)S(1)}, f32[128]{0:T(128)}, u32[]{:S(2)}) copy-start(f32[128]{0:T(128)} %param.21) | copy-start | bytes 1540
  (2 other events, 1.9 us)
Sparse Core Ops, SparseCore 0:
  198.1 194.3 all-gather.4
  395.8 189.7 all-gather.6
  649.0 106.4 all-reduce.1
  758.3 6.8 reduce-scatter.1
where the time goes:
time: 773 us; the launch traced here: 772 us
  waiting for transfers between devices  489 us (63%)
  other arithmetic  167 us (22%)
  matrix products  84.4 us (11%)
  local copies, waits for them, and re-layouts  16.2 us (2%)
  between operations  14.2 us (2%)
    all_gather x2, waiting for transfers between devices, prefix(): pieces = jax.tree.map(lambda part: lax.all_gather(part, axis), value)  381 us
    another operation x4, other arithmetic, prepare(): lax.linalg.triangular_solve(system, right_side, left_side=True, lower=Tru...  158 us
    psum x1, waiting for transfers between devices, from_root(): return lax.psum(jnp.where(mine, value, jnp.zeros_like(value)), axis)  100 us
    dot_general x19, matrix products, compose_maps(): jnp.einsum('...ij,...jk->...ik', first_map, second_map, precision=PRECISE)  49 us
  transfers between devices with their start and end apart: 4, of which 4 were waited for; matrix products, arithmetic and copies ran while one was open for 2% of the time, Pallas kernels for 0%

commit v1 on v0

v1 whole, which is shorter than its diff:
```python
import functools

import jax
import jax.numpy as jnp
from jax import lax
from jax.experimental import pallas as pl
from jax.experimental.pallas import tpu as pltpu
from jax.sharding import PartitionSpec as P

DK = 128
DV = 128
SMALL = 16
HIGH = lax.Precision.HIGHEST
F32 = jnp.float32
BF16 = jnp.bfloat16
VMEM_LIMIT = 48 * 1024 * 1024

NN = (((1,), (0,)), ((), ()))
NT = (((1,), (1,)), ((), ()))
TN = (((0,), (0,)), ((), ()))


def dot(a, b, dims=NN, precision=None):
    return lax.dot_general(a, b, dims, precision=precision, preferred_element_type=F32)


def split(x):
    high = x.astype(BF16)
    return high, (x - high.astype(F32)).astype(BF16)


def dot3(a, b):
    a_high, a_low = a
    b_high, b_low = b
    return dot(a_high, b_high) + (dot(a_high, b_low) + dot(a_low, b_high))


def row_col(size):
    return (
        lax.broadcasted_iota(jnp.int32, (size, size), 0),
        lax.broadcasted_iota(jnp.int32, (size, size), 1),
    )


def maps_kernel(k_ref, v_ref, g_ref, b_ref, pair_ref, solved_ref, l_scr, d_scr, t_scr):
    tokens = k_ref.shape[1]
    heads = g_ref.shape[1]
    repeat = heads // (k_ref.shape[2] // DK)
    blocks = tokens // SMALL
    row, col = row_col(tokens)
    lower = row >= col
    strict = row > col
    eye = row == col
    same_small = (row // SMALL) == (col // SMALL)
    gates = g_ref[0]
    betas = b_ref[0]
    tri = jnp.where(lower, 1.0, 0.0)
    cum_cols = dot(tri, gates, NT, HIGH)
    cum_rows = dot(gates, tri, NT, HIGH)
    beta_cols = dot(jnp.where(eye, 1.0, 0.0), betas, NT, HIGH)
    pick = jnp.where(
        lax.broadcasted_iota(jnp.int32, (tokens, DK), 0) % SMALL
        == lax.broadcasted_iota(jnp.int32, (tokens, DK), 1),
        1.0,
        0.0,
    ).astype(BF16)
    unit = [
        jnp.where(
            lax.broadcasted_iota(jnp.int32, (blocks, tokens), 1)
            == lax.broadcasted_iota(jnp.int32, (blocks, tokens), 0) * SMALL + i,
            1.0,
            0.0,
        )
        for i in range(SMALL)
    ]
    systems = []
    key_cols, key_rows = [], []
    for h in range(heads):
        kh = h // repeat
        if h % repeat == 0:
            key = k_ref[0, :, kh * DK : (kh + 1) * DK]
            gram = dot(key, key, NT)
            on_diag = jnp.where(eye, gram, 0.0)
            key_cols.append(lax.rsqrt(jnp.sum(on_diag, axis=1, keepdims=True) + 1e-6))
            key_rows.append(lax.rsqrt(jnp.sum(on_diag, axis=0, keepdims=True) + 1e-6))
        decay = jnp.exp(jnp.where(strict, cum_cols[:, h : h + 1] - cum_rows[h : h + 1, :], -1e30))
        system = decay * gram * (beta_cols[:, h : h + 1] * key_cols[kh]) * key_rows[kh]
        systems.append(system)
        high, low = split(jnp.where(same_small, system, 0.0))
        d_scr[h] = dot(high, pick) + dot(low, pick)
    for h in range(heads):
        rows = [unit[0]]
        for i in range(1, SMALL):
            coef = d_scr[h, pl.ds(i, blocks, stride=SMALL), :]
            value = unit[i]
            for j in range(i):
                value = value - coef[:, j : j + 1] * rows[j]
            rows.append(value)
        for i in range(SMALL):
            t_scr[h, pl.ds(i, blocks, stride=SMALL), :] = rows[i]
    inverse = [t_scr[h] for h in range(heads)]
    size = SMALL
    while size < tokens:
        mask = jnp.logical_and((row // (2 * size)) == (col // (2 * size)), (row // size) != (col // size))
        parts = [split(t) for t in inverse]
        inner = [dot3(split(jnp.where(mask, systems[h], 0.0)), parts[h]) for h in range(heads)]
        inverse = [inverse[h] - dot3(parts[h], split(inner[h])) for h in range(heads)]
        size *= 2
    for h in range(heads):
        kh = h // repeat
        key = k_ref[0, :, kh * DK : (kh + 1) * DK]
        scaled = inverse[h] * betas[h : h + 1, :]
        update = dot(scaled.astype(BF16), v_ref[0, :, h * DV : (h + 1) * DV])
        erase = dot((scaled * (jnp.exp(cum_rows[h : h + 1, :]) * key_rows[kh])).astype(BF16), key)
        last = cum_rows[h : h + 1, tokens - 1 :]
        weight = jnp.exp(last - cum_cols[:, h : h + 1]) * key_cols[kh]
        both = jnp.concatenate([erase, update], axis=1)
        solved_ref[h] = both.astype(BF16)
        moved = dot(key, (both * weight).astype(BF16), TN)
        gone = moved[:, :DK] + jnp.where(eye[:DK, :DK], 1.0 - jnp.exp(last), 0.0)
        pair_ref[h] = jnp.concatenate([gone, moved[:, DK:]], axis=1).astype(BF16)


def mix_kernel(q_ref, k_ref, z_ref, g_ref, gain_ref, solved_ref, query_ref, intra_ref, gate_ref):
    tokens = k_ref.shape[1]
    heads = g_ref.shape[1]
    repeat = heads // (k_ref.shape[2] // DK)
    row, col = row_col(tokens)
    lower = row >= col
    eye = row == col
    gates = g_ref[0]
    tri = jnp.where(lower, 1.0, 0.0)
    cum_cols = dot(tri, gates, NT, HIGH)
    cum_rows = dot(gates, tri, NT, HIGH)
    gain = gain_ref[0:1, :]
    ones = jnp.ones((8, DK), BF16)
    for h in range(heads):
        kh = h // repeat
        if h % repeat == 0:
            key = k_ref[0, :, kh * DK : (kh + 1) * DK]
            query = q_ref[0, :, kh * DK : (kh + 1) * DK]
            keyf = key.astype(F32)
            square_high, square_low = split(keyf * keyf)
            key_row = lax.rsqrt((dot(ones, square_high, NT) + dot(ones, square_low, NT))[0:1] + 1e-6)
            queryf = query.astype(F32)
            query_col = lax.rsqrt(jnp.sum(queryf * queryf, axis=1, keepdims=True) + 1e-6) * DK**-0.5
            product = dot(query, key, NT) * query_col * key_row
        decay = jnp.exp(jnp.where(lower, cum_cols[:, h : h + 1] - cum_rows[h : h + 1, :], -1e30))
        mixed = dot((decay * product).astype(BF16), solved_ref[h])
        intra_ref[:, h * DV : (h + 1) * DV] = mixed[:, DK:]
        reach = jnp.exp(cum_cols[:, h : h + 1]) * query_col
        query_ref[:, h * DK : (h + 1) * DK] = (reach * queryf - mixed[:, :DK]).astype(BF16)
        z = z_ref[0, :, h * DV : (h + 1) * DV].astype(F32)
        gate_ref[:, h * DV : (h + 1) * DV] = gain * z / (1.0 + jnp.exp(-z))


def chain_kernel(pair_ref, start_ref, entry_ref, exit_ref):
    count, heads = pair_ref.shape[0], pair_ref.shape[1]
    states = [start_ref[h].astype(F32) for h in range(heads)]
    for j in range(count):
        for h in range(heads):
            high, low = split(states[h])
            entry_ref[j, h] = high
            moved = dot(pair_ref[j, h, :, :DK], jnp.concatenate([high, low], axis=1))
            states[h] = states[h] - (moved[:, :DV] + moved[:, DV:]) + pair_ref[j, h, :, DK:].astype(F32)
    for h in range(heads):
        exit_ref[h] = states[h].astype(BF16)


def read_kernel(query_ref, intra_ref, gate_ref, entry_ref, w_ref, out_ref, normed_scr):
    heads = entry_ref.shape[0]

    @pl.when(pl.program_id(0) == 0)
    def _():
        for h in range(heads):
            cols = slice(h * DV, (h + 1) * DV)
            value = intra_ref[:, cols] + dot(query_ref[:, cols], entry_ref[h])
            scale = lax.rsqrt(jnp.mean(value * value, axis=1, keepdims=True) + 1e-6)
            normed_scr[:, cols] = (value * scale * gate_ref[:, cols]).astype(BF16)

    out_ref[...] = dot(normed_scr[...], w_ref[...]).astype(BF16)


def params():
    return pltpu.CompilerParams(vmem_limit_bytes=VMEM_LIMIT)


def shard_maps(keys, values, log_decay, beta):
    tokens, heads, key_heads = keys.shape[1], log_decay.shape[1], keys.shape[2] // DK
    step = min(8, heads)
    key_step = step * key_heads // heads
    shape = jax.ShapeDtypeStruct((heads, tokens, DK + DV), BF16)
    pair = jax.ShapeDtypeStruct((heads, DK, DK + DV), BF16)
    return pl.pallas_call(
        maps_kernel,
        grid=(heads // step,),
        in_specs=[
            pl.BlockSpec((1, tokens, key_step * DK), lambda i: (0, 0, i)),
            pl.BlockSpec((1, tokens, step * DV), lambda i: (0, 0, i)),
            pl.BlockSpec((1, step, tokens), lambda i: (0, i, 0)),
            pl.BlockSpec((1, step, tokens), lambda i: (0, i, 0)),
        ],
        out_specs=[
            pl.BlockSpec((step, DK, DK + DV), lambda i: (i, 0, 0)),
            pl.BlockSpec((step, tokens, DK + DV), lambda i: (i, 0, 0)),
        ],
        out_shape=[pair, shape],
        scratch_shapes=[
            pltpu.VMEM((step, tokens, tokens), F32),
            pltpu.VMEM((step, tokens, DK), F32),
            pltpu.VMEM((step, tokens, tokens), F32),
        ],
        compiler_params=params(),
        name="shard_maps",
    )(keys, values, log_decay, beta)


def local_mix(queries, keys, out_gate, log_decay, gain, solved):
    tokens, heads, key_heads = keys.shape[1], log_decay.shape[1], keys.shape[2] // DK
    step = min(8, heads)
    key_step = step * key_heads // heads
    wide = pl.BlockSpec((tokens, step * DV), lambda i: (0, i))
    return pl.pallas_call(
        mix_kernel,
        grid=(heads // step,),
        in_specs=[
            pl.BlockSpec((1, tokens, key_step * DK), lambda i: (0, 0, i)),
            pl.BlockSpec((1, tokens, key_step * DK), lambda i: (0, 0, i)),
            pl.BlockSpec((1, tokens, step * DV), lambda i: (0, 0, i)),
            pl.BlockSpec((1, step, tokens), lambda i: (0, i, 0)),
            pl.BlockSpec((1, DV), lambda i: (0, 0)),
            pl.BlockSpec((step, tokens, DK + DV), lambda i: (i, 0, 0)),
        ],
        out_specs=[wide, wide, wide],
        out_shape=[
            jax.ShapeDtypeStruct((tokens, heads * DK), BF16),
            jax.ShapeDtypeStruct((tokens, heads * DV), F32),
            jax.ShapeDtypeStruct((tokens, heads * DV), F32),
        ],
        compiler_params=params(),
        cost_estimate=pl.CostEstimate(flops=heads * 10 * 128**3, bytes_accessed=4 << 20, transcendentals=0),
        name="local_mix",
    )(queries, keys, out_gate, log_decay, gain, solved)


def run_chain(pairs, start):
    count, heads = pairs.shape[0], pairs.shape[1]
    return pl.pallas_call(
        chain_kernel,
        out_shape=[
            jax.ShapeDtypeStruct((count, heads, DK, DV), BF16),
            jax.ShapeDtypeStruct((heads, DK, DV), BF16),
        ],
        compiler_params=params(),
        name="chain",
    )(pairs, start)


def read_out(query, intra, gate, entry, weight):
    tokens, width = query.shape
    columns = weight.shape[1]
    step = min(512, columns)
    whole = lambda i: (0, 0)
    return pl.pallas_call(
        read_kernel,
        grid=(columns // step,),
        in_specs=[
            pl.BlockSpec((tokens, width), whole),
            pl.BlockSpec((tokens, width), whole),
            pl.BlockSpec((tokens, width), whole),
            pl.BlockSpec(entry.shape, lambda i: (0, 0, 0)),
            pl.BlockSpec((width, step), lambda i: (0, i)),
        ],
        out_specs=pl.BlockSpec((tokens, step), lambda i: (0, i)),
        out_shape=jax.ShapeDtypeStruct((tokens, columns), BF16),
        scratch_shapes=[pltpu.VMEM((tokens, width), BF16)],
        compiler_params=params(),
        name="read_out",
    )(query, intra, gate, entry, weight)


def group_size(count, heads):
    return max(s for s in range(1, 9) if count % s == 0 and heads % s == 0)


def local(queries, keys, values, out_gate, log_decay, beta, norm_gain, out_weight, owner):
    tokens, heads = keys.shape[1], log_decay.shape[1]
    count = lax.axis_size("seq")
    me = lax.axis_index("seq")
    size = group_size(count, heads)
    groups = count // size
    own = heads // size
    members = [[g * size + i for i in range(size)] for g in range(groups)]

    def swap(x):
        return lax.all_to_all(x, "seq", 0, 0, axis_index_groups=members, tiled=True)

    def hop(x, source, target):
        return lax.ppermute(x, "seq", [(source * size + i, target * size + i) for i in range(size)])

    pair, solved = shard_maps(keys, values, log_decay, beta)
    pairs = swap(pair.reshape(size, own, DK, DK + DV))
    query, intra, gate = local_mix(queries, keys, out_gate, log_decay, norm_gain[None], solved)
    start = jnp.zeros((own, DK, DV), BF16)
    for g in range(groups - 1):
        _, leave = run_chain(pairs, start)
        start = start + hop(leave, g, g + 1)
    entries, leave = run_chain(pairs, start)
    entry = swap(entries).reshape(heads, DK, DV)
    last = jnp.where(me // size == groups - 1, leave, jnp.zeros_like(leave))
    for g in range(groups - 1, 0, -1):
        last = last + hop(last, g, g - 1)
    mine = lax.dynamic_slice_in_dim(owner[0], (me % size) * own, own)
    to = (me // size) * size + jnp.arange(size, dtype=jnp.int32)
    kept = (mine[None, :] == to[:, None])[:, :, None, None]
    finals = swap(jnp.where(kept, last[None], jnp.zeros_like(last)[None]))
    decode_states = finals.reshape(1, heads, DK, DV).astype(F32)
    partial_value = read_out(query, intra, gate, entry, out_weight)
    ranks = lax.axis_size("head")
    if ranks == 2:
        half = tokens // 2
        rank = lax.axis_index("head")
        keep = lax.dynamic_slice_in_dim(partial_value, rank * half, half)
        give = lax.dynamic_slice_in_dim(partial_value, (1 - rank) * half, half)
        got = lax.ppermute(give, "head", [(0, 1), (1, 0)])
        total = (keep.astype(F32) + got.astype(F32)).astype(BF16)
    else:
        total = lax.psum_scatter(partial_value, "head", scatter_dimension=0, tiled=True)
    return (total[:, None, :], decode_states)


def solution(mesh):
    placed = (
        P(None, "seq", "head"),
        P(None, "seq", "head"),
        P(None, "seq", "head"),
        P(None, "seq", "head"),
        P(None, "head", "seq"),
        P(None, "head", "seq"),
        P(),
        P("head", None),
        P(None, "head"),
    )
    return jax.shard_map(
        local,
        mesh=mesh,
        in_specs=placed,
        out_specs=(P(("seq", "head"), None, None), P("seq", "head", None, None)),
        check_vma=False,
    )
```

time: 773 us -> 80.4 us (0.10)
  waiting for transfers between devices: 489 us -> 24.4 us
  other arithmetic: 167 us -> 3.89 us
  matrix products: 84.4 us -> 0 us
  Pallas kernels: 0 us -> 23.6 us
  starting transfers between devices: 0.16 us -> 22.2 us
  between operations: 14.2 us -> 0.76 us
  local copies, waits for them, and re-layouts: 16.2 us -> 4.87 us
    all_gather x2 -> x0, waiting for transfers between devices: 381 us -> none  [prefix(): pieces = jax.tree.map(lambda part: lax.all_gather(part, axis), value)]
    another operation x5 -> x0, other arithmetic: 159 us -> none  [the longest x4 158 us: prepare(): lax.linalg.triangular_solve(system, right_side, left_side=True, lower=Tru...]
    psum x1 -> x0, waiting for transfers between devices: 100 us -> none  [from_root(): return lax.psum(jnp.where(mine, value, jnp.zeros_like(value)), axis)]
    dot_general x32 -> x0, matrix products: 82 us -> none  [the longest x19 49 us: compose_maps(): jnp.einsum('...ij,...jk->...ik', first_map, second_map, precision=PRECISE)]
    pallas_call x0 -> x5, Pallas kernels: none -> 23.6 us  [the longest x1 11.5 us: shard_maps(): pl.pallas_call(maps_kernel, grid=(heads // step,), in_specs=[pl.BlockSpec...]
    all_to_all x0 -> x3, waiting for transfers between devices: none -> 16.8 us  [swap(): return lax.all_to_all(x, 'seq', 0, 0, axis_index_groups=members, tiled=True)]
    all_to_all x0 -> x3, starting transfers between devices: none -> 16.3 us  [swap(): return lax.all_to_all(x, 'seq', 0, 0, axis_index_groups=members, tiled=True)]
    while x36 -> x0, local copies, waits for them, and re-layouts: 8.36 us -> none
  transfers between devices with their start and end apart: 4 -> 6, of which waited for: 4 -> 4; matrix products, arithmetic and copies ran while one was open for 2% -> 4% of each run, Pallas kernels for 0% -> 10%
where the time goes in v1:
time: 80.4 us; the launch traced here: 79.8 us
  waiting for transfers between devices  24.4 us (30%)
  Pallas kernels  23.6 us (29%)
  starting transfers between devices  22.2 us (28%)
  local copies, waits for them, and re-layouts  4.87 us (6%)
  other arithmetic  3.89 us (5%)
    all_to_all x3, waiting for transfers between devices, swap(): return lax.all_to_all(x, 'seq', 0, 0, axis_index_groups=members, tiled=True)  16.8 us
    all_to_all x3, starting transfers between devices, swap(): return lax.all_to_all(x, 'seq', 0, 0, axis_index_groups=members, tiled=True)  16.3 us
    pallas_call x1, Pallas kernels, shard_maps(): pl.pallas_call(maps_kernel, grid=(heads // step,), in_specs=[pl.BlockSpec...  11.5 us
    ppermute x2, waiting for transfers between devices, hop(): lax.ppermute(x, 'seq', [(source * size + i, target * size + i) for i in r...  7.58 us
    ppermute x2, starting transfers between devices, hop(): lax.ppermute(x, 'seq', [(source * size + i, target * size + i) for i in r...  5.78 us
    pallas_call x1, Pallas kernels, read_out(): pl.pallas_call(read_kernel, grid=(columns // step,), in_specs=[pl.BlockSp...  5.45 us
    unnamed x20, local copies, waits for them, and re-layouts  4.75 us
    pallas_call x2, Pallas kernels, run_chain(): pl.pallas_call(chain_kernel, out_shape=[jax.ShapeDtypeStruct((count, head...  3.94 us
  transfers between devices with their start and end apart: 6, of which 4 were waited for; matrix products, arithmetic and copies ran while one was open for 4% of the time, Pallas kernels for 10%

profile of v1, /device:TPU:0, one launch (start us, length us, event | category | flops | bytes accessed | tf_op | source)
XLA Modules:
  0.0 79.8 jit_solution(3058883606066899834)
XLA Ops:
  0.7 0.9 %copy-done.1 = bf16[1,128,1024]{2,1,0:T(8,128)(2,1)S(1)} copy-done((bf16[1,128,1024]{2,1,0:T(8,128)(2,1)S(1)}, bf16[1,128,1024]{2,1,0:T(8,128)(2,1)}, u32[]{:S(2)}) %copy-start.1) | copy-done | bytes 262168
  1.6 1.0 %copy-done.4 = bf16[1,128,2048]{2,1,0:T(8,128)(2,1)S(1)} copy-done((bf16[1,128,2048]{2,1,0:T(8,128)(2,1)S(1)}, bf16[1,128,2048]{2,1,0:T(8,128)(2,1)}, u32[]{:S(2)}) %copy-start.4) | copy-done | bytes 524312
  2.6 0.7 copy-done.6
  3.3 0.7 copy-done.8
  4.0 11.5 %shard_maps.1 = (bf16[16,128,256]{2,1,0:T(8,128)(2,1)}, bf16[16,128,256]{2,1,0:T(8,128)(2,1)S(1)}) custom-call(bf16[1,128,1024]{2,1,0:T(8,128)(2,1)S(1)} %copy-done.1, bf16[1,128,2048]{2,1,0:T(8,128)(2,1)S(1)} %copy-done.4, f32[1,16,128]{2,1,0:T(8,128)S(1)} %copy-done.6, f32[1,16,128]{2,1,0:T(8,128)S(1)} %copy-done.8), custom_call_target="tpu_custom_call" | custom-call | tf_op jit(solution)/shard_map/shard_maps/pallas_call | solution.py:194
  15.6 6.2 %all-to-all-start = ((bf16[8,2,128,256]{3,2,1,0:T(8,128)(2,1)}), bf16[8,2,128,256]{3,2,1,0:T(8,128)(2,1)S(1)}, u32[]{:S(2)}, u32[]{:S(2)}) async-start(bf16[8,2,128,256]{3,2,1,0:T(8,128)(2,1)} %bitcast.1), calls=%async_computation | async-start | bytes 2097152 | tf_op jit(solution)/shard_map/all_to_all | solution.py:296
  21.8 14.7 %all-to-all-done.pair_ref = bf16[8,2,128,256]{3,2,1,0:T(8,128)(2,1)S(1)} async-done(((bf16[8,2,128,256]{3,2,1,0:T(8,128)(2,1)}), bf16[8,2,128,256]{3,2,1,0:T(8,128)(2,1)S(1)}, u32[]{:S(2)}, u32[]{:S(2)}) %all-to-all-start) | async-done | bytes 1048608 | tf_op jit(solution)/shard_map/all_to_all | solution.py:296
  36.5 2.0 %chain.2 = (bf16[8,2,128,128]{3,2,1,0:T(8,128)(2,1)}, bf16[2,128,128]{2,1,0:T(8,128)(2,1)S(1)}) custom-call(bf16[8,2,128,256]{3,2,1,0:T(8,128)(2,1)S(1)} %all-to-all-done.pair_ref, bf16[2,128,128]{2,1,0:T(8,128)(2,1)S(1)} %broadcast_1_start_ref.2.start_ref), custom_call_target="tpu_custom_call" | custom-call | tf_op jit(solution)/shard_map/chain/pallas_call | solution.py:248
  38.4 4.5 %collective-permute-start = (bf16[2,128,128]{2,1,0:T(8,128)(2,1)S(1)}, bf16[2,128,128]{2,1,0:T(8,128)(2,1)S(1)}, u32[]{:S(2)}, u32[]{:S(2)}) collective-permute-start(bf16[2,128,128]{2,1,0:T(8,128)(2,1)S(1)} %get-tuple-element.15), channel_id=1, source_target_pairs={{0,16},{2,18},{4,20},{6,22},{8,24},{10,26},{12,28},{14,30},{1,17},... | collective-permute-start | bytes 196616 | tf_op jit(solution)/shard_map/ppermute | solution.py:299
  43.0 0.1 fusion.1
  43.0 1.8 %collective-permute-done.start_ref = bf16[2,128,128]{2,1,0:T(8,128)(2,1)S(1)} collective-permute-done((bf16[2,128,128]{2,1,0:T(8,128)(2,1)S(1)}, bf16[2,128,128]{2,1,0:T(8,128)(2,1)S(1)}, u32[]{:S(2)}, u32[]{:S(2)}) %collective-permute-start) | collective-permute-done | bytes 65568 | tf_op jit(solution)/shard_map/ppermute | solution.py:299
  44.8 2.0 %chain.3 = (bf16[8,2,128,128]{3,2,1,0:T(8,128)(2,1)}, bf16[2,128,128]{2,1,0:T(8,128)(2,1)S(1)}) custom-call(bf16[8,2,128,256]{3,2,1,0:T(8,128)(2,1)S(1)} %all-to-all-done.pair_ref, bf16[2,128,128]{2,1,0:T(8,128)(2,1)S(1)} %collective-permute-done.start_ref), custom_call_target="tpu_custom_call" | custom-call | tf_op jit(solution)/shard_map/chain/pallas_call | solution.py:248
  46.8 3.9 %all-to-all-start.1 = ((bf16[8,2,128,128]{3,2,1,0:T(8,128)(2,1)}), bf16[8,2,128,128]{3,2,1,0:T(8,128)(2,1)S(1)}, u32[]{:S(2)}, u32[]{:S(2)}) async-start(bf16[8,2,128,128]{3,2,1,0:T(8,128)(2,1)} %get-tuple-element.16), calls=%async_computation.1 | async-start | bytes 1048576 | tf_op jit(solution)/shard_map/all_to_all | solution.py:296
  50.7 1.3 %collective-permute-start.2 = (bf16[2,128,128]{2,1,0:T(8,128)(2,1)S(1)}, bf16[2,128,128]{2,1,0:T(8,128)(2,1)S(1)}, u32[]{:S(2)}, u32[]{:S(2)}) collective-permute-start(bf16[2,128,128]{2,1,0:T(8,128)(2,1)S(1)} %broadcast_select_fusion.1), channel_id=1, source_target_pairs={{16,0},{18,2},{20,4},{22,6},{24,8},{26,10},{28,12},{30,14},{17,1},... | collective-permute-start | bytes 196616 | tf_op jit(solution)/shard_map/ppermute | solution.py:299
  52.0 5.8 %collective-permute-done.2 = bf16[2,128,128]{2,1,0:T(8,128)(2,1)S(1)} collective-permute-done((bf16[2,128,128]{2,1,0:T(8,128)(2,1)S(1)}, bf16[2,128,128]{2,1,0:T(8,128)(2,1)S(1)}, u32[]{:S(2)}, u32[]{:S(2)}) %collective-permute-start.2) | collective-permute-done | bytes 65568 | tf_op jit(solution)/shard_map/ppermute | solution.py:299
  57.8 0.9 %broadcast_select_fusion = bf16[8,2,128,128]{3,2,1,0:T(8,128)(2,1)} fusion(pred[8,2]{1,0:T(8,128)(4,1)S(1)} %broadcast_compare_fusion, bf16[2,128,128]{2,1,0:T(8,128)(2,1)S(1)} %fusion.2), kind=kLoop, calls=%fused_computation.2 | loop fusion | flops 262144 | bytes 589840 | tf_op jit(solution)/shard_map/jit(_where)/select_n | solution.py:316
  58.7 2.2 %all-to-all-done.1 = bf16[8,2,128,128]{3,2,1,0:T(8,128)(2,1)S(1)} async-done(((bf16[8,2,128,128]{3,2,1,0:T(8,128)(2,1)}), bf16[8,2,128,128]{3,2,1,0:T(8,128)(2,1)S(1)}, u32[]{:S(2)}, u32[]{:S(2)}) %all-to-all-start.1) | async-done | bytes 524320 | tf_op jit(solution)/shard_map/all_to_all | solution.py:296
  60.9 6.3 %all-to-all-start.2 = ((bf16[8,2,128,128]{3,2,1,0:T(8,128)(2,1)}), bf16[8,2,128,128]{3,2,1,0:T(8,128)(2,1)}, u32[]{:S(2)}, u32[]{:S(2)}) async-start(bf16[8,2,128,128]{3,2,1,0:T(8,128)(2,1)} %broadcast_select_fusion), calls=%async_computation.2 | async-start | bytes 1048576 | tf_op jit(solution)/shard_map/all_to_all | solution.py:296
  67.2 0.7 copy-done.7
  67.9 0.7 copy-done.9
  68.6 2.7 %local_mix.1 = (bf16[128,2048]{1,0:T(8,128)(2,1)S(1)}, f32[128,2048]{1,0:T(8,128)S(1)}, f32[128,2048]{1,0:T(8,128)S(1)}) custom-call(bf16[1,128,1024]{2,1,0:T(8,128)(2,1)S(1)} %copy-done.5, bf16[1,128,1024]{2,1,0:T(8,128)(2,1)S(1)} %copy-done.2, bf16[1,128,2048]{2,1,0:T(8,128)(2,1)S(1)} %copy-done.3, f32[1,16,128]{2,1,0:T(8,128)S(1)} %copy-done.7, ...), custom_call_target="tpu_custom_call" | custom-call | flops 335544320 | bytes 4194304 | tf_op jit(solution)/shard_map/local_mix/pallas_call | solution.py:223
  71.3 5.5 %read_out.1 = bf16[128,2048]{1,0:T(8,128)(2,1)S(1)} custom-call(bf16[128,2048]{1,0:T(8,128)(2,1)S(1)} %get-tuple-element.11.query_ref, f32[128,2048]{1,0:T(8,128)S(1)} %get-tuple-element.12.intra_ref, f32[128,2048]{1,0:T(8,128)S(1)} %get-tuple-element.13.gate_ref, bf16[16,128,128]{2,1,0:T(8,128)(2,1)S(1)} %bitcast.11, bf16[2048,2048]{1,0:T(8,128)(2,1)} %w_ref.1), custom_call_target="tpu_custom_call" | custom-call | tf_op jit(solution)/shard_map/read_out/pallas_call | solution.py:264
  76.9 2.1 %bitcast_convert_fusion = f32[1,16,128,128]{3,2,1,0:T(8,128)} fusion(bf16[1,16,128,128]{3,2,1,0:T(8,128)(2,1)} %bitcast.10), kind=kLoop, calls=%fused_computation | loop fusion | flops 262144 | bytes 1572864 | tf_op jit(solution)/shard_map/convert_element_type | solution.py:317
  79.0 0.8 fusion
  (23 shorter events, 0.2 us)
Async XLA Ops:
  0.6 42.3 %copy-start = (s32[1,16]{1,0:T(1,128)S(1)}, s32[1,16]{1,0:T(1,128)}, u32[]{:S(2)}) copy-start(s32[1,16]{1,0:T(1,128)} %param.17) | copy-start | bytes 196
  0.6 1.0 %copy-start.1 = (bf16[1,128,1024]{2,1,0:T(8,128)(2,1)S(1)}, bf16[1,128,1024]{2,1,0:T(8,128)(2,1)}, u32[]{:S(2)}) copy-start(bf16[1,128,1024]{2,1,0:T(8,128)(2,1)} %k_ref.3) | copy-start | bytes 786436
  1.6 1.0 %copy-start.4 = (bf16[1,128,2048]{2,1,0:T(8,128)(2,1)S(1)}, bf16[1,128,2048]{2,1,0:T(8,128)(2,1)}, u32[]{:S(2)}) copy-start(bf16[1,128,2048]{2,1,0:T(8,128)(2,1)} %v_ref.1) | copy-start | bytes 1572868
  2.6 0.7 copy-start.6
  3.3 0.7 copy-start.8
  4.0 63.2 %copy-start.2 = (bf16[1,128,1024]{2,1,0:T(8,128)(2,1)S(1)}, bf16[1,128,1024]{2,1,0:T(8,128)(2,1)}, u32[]{:S(2)}) copy-start(bf16[1,128,1024]{2,1,0:T(8,128)(2,1)} %k_ref.3) | copy-start | bytes 786436
  4.0 63.2 %copy-start.3 = (bf16[1,128,2048]{2,1,0:T(8,128)(2,1)S(1)}, bf16[1,128,2048]{2,1,0:T(8,128)(2,1)}, u32[]{:S(2)}) copy-start(bf16[1,128,2048]{2,1,0:T(8,128)(2,1)} %z_ref.1) | copy-start | bytes 1572868
  4.0 63.2 %copy-start.5 = (bf16[1,128,1024]{2,1,0:T(8,128)(2,1)S(1)}, bf16[1,128,1024]{2,1,0:T(8,128)(2,1)}, u32[]{:S(2)}) copy-start(bf16[1,128,1024]{2,1,0:T(8,128)(2,1)} %q_ref.1) | copy-start | bytes 786436
  15.6 20.9 %all-to-all-start = ((bf16[8,2,128,256]{3,2,1,0:T(8,128)(2,1)}), bf16[8,2,128,256]{3,2,1,0:T(8,128)(2,1)S(1)}, u32[]{:S(2)}, u32[]{:S(2)}) async-start(bf16[8,2,128,256]{3,2,1,0:T(8,128)(2,1)} %bitcast.1), calls=%async_computation | async-start | bytes 2097152 | tf_op jit(solution)/shard_map/all_to_all | solution.py:296
  38.4 6.4 %collective-permute-start = (bf16[2,128,128]{2,1,0:T(8,128)(2,1)S(1)}, bf16[2,128,128]{2,1,0:T(8,128)(2,1)S(1)}, u32[]{:S(2)}, u32[]{:S(2)}) collective-permute-start(bf16[2,128,128]{2,1,0:T(8,128)(2,1)S(1)} %get-tuple-element.15), channel_id=1, source_target_pairs={{0,16},{2,18},{4,20},{6,22},{8,24},{10,26},{12,28},{14,30},{1,17},... | collective-permute-start | bytes 196616 | tf_op jit(solution)/shard_map/ppermute | solution.py:299
  46.8 14.1 %all-to-all-start.1 = ((bf16[8,2,128,128]{3,2,1,0:T(8,128)(2,1)}), bf16[8,2,128,128]{3,2,1,0:T(8,128)(2,1)S(1)}, u32[]{:S(2)}, u32[]{:S(2)}) async-start(bf16[8,2,128,128]{3,2,1,0:T(8,128)(2,1)} %get-tuple-element.16), calls=%async_computation.1 | async-start | bytes 1048576 | tf_op jit(solution)/shard_map/all_to_all | solution.py:296
  50.7 7.2 %collective-permute-start.2 = (bf16[2,128,128]{2,1,0:T(8,128)(2,1)S(1)}, bf16[2,128,128]{2,1,0:T(8,128)(2,1)S(1)}, u32[]{:S(2)}, u32[]{:S(2)}) collective-permute-start(bf16[2,128,128]{2,1,0:T(8,128)(2,1)S(1)} %broadcast_select_fusion.1), channel_id=1, source_target_pairs={{16,0},{18,2},{20,4},{22,6},{24,8},{26,10},{28,12},{30,14},{17,1},... | collective-permute-start | bytes 196616 | tf_op jit(solution)/shard_map/ppermute | solution.py:299
  60.9 15.9 %all-to-all-start.2 = ((bf16[8,2,128,128]{3,2,1,0:T(8,128)(2,1)}), bf16[8,2,128,128]{3,2,1,0:T(8,128)(2,1)}, u32[]{:S(2)}, u32[]{:S(2)}) async-start(bf16[8,2,128,128]{3,2,1,0:T(8,128)(2,1)} %broadcast_select_fusion), calls=%async_computation.2 | async-start | bytes 1048576 | tf_op jit(solution)/shard_map/all_to_all | solution.py:296
  67.2 0.7 copy-start.7
  67.9 0.7 copy-start.9
  76.8 2.2 %collective-permute-start.1 = (bf16[64,2048]{1,0:T(8,128)(2,1)S(1)}, bf16[64,2048]{1,0:T(8,128)(2,1)S(1)}, u32[]{:S(2)}, u32[]{:S(2)}) collective-permute-start(bf16[64,2048]{1,0:T(8,128)(2,1)S(1)} %constant_dynamic-slice_fusion.1), channel_id=1, source_target_pairs={{0,1},{1,0},{2,3},{3,2},{4,5},{5,4},{6,7},{7,6},{8,9},{9,8},{10,11... | collective-permute-start | bytes 786440 | tf_op jit(solution)/shard_map/ppermute | solution.py:325

commit v2 on v1

v2 whole, which is shorter than its diff:
```python
import jax
import jax.numpy as jnp
from jax import lax
from jax.experimental import pallas as pl
from jax.experimental.pallas import tpu as pltpu
from jax.sharding import PartitionSpec as P

DK = 128
DV = 128
SMALL = 16
EXTRA = 16
HIGH = lax.Precision.HIGHEST
F32 = jnp.float32
BF16 = jnp.bfloat16
VMEM_LIMIT = 40 * 1024 * 1024
VMEM_MOST = 63 * 1024 * 1024
VMEM_WIDE = 50 * 1024 * 1024
VMEM_LEAST = 4 * 1024 * 1024

NN = (((1,), (0,)), ((), ()))
NT = (((1,), (1,)), ((), ()))
TN = (((0,), (0,)), ((), ()))


def dot(a, b, dims=NN, precision=None):
    return lax.dot_general(a, b, dims, precision=precision, preferred_element_type=F32)


def split(x):
    high = x.astype(BF16)
    return high, (x - high.astype(F32)).astype(BF16)


def dot3(a, b):
    width = b[0].shape[1]
    both = dot(a[0], jnp.concatenate(b, axis=1))
    return both[:, :width] + (both[:, width:] + dot(a[1], b[0]))


def row_col(size):
    return (
        lax.broadcasted_iota(jnp.int32, (size, size), 0),
        lax.broadcasted_iota(jnp.int32, (size, size), 1),
    )


def inverses(systems, d_scr, t_scr):
    count, tokens = len(systems), systems[0].shape[0]
    blocks = tokens // SMALL
    row, col = row_col(tokens)
    same_small = (row // SMALL) == (col // SMALL)
    pick = jnp.where((row % SMALL) == col, 1.0, 0.0).astype(BF16)
    lane = lax.broadcasted_iota(jnp.int32, (blocks, tokens), 1)
    first = lax.broadcasted_iota(jnp.int32, (blocks, tokens), 0) * SMALL
    unit = [jnp.where(lane == first + i, 1.0, 0.0) for i in range(SMALL)]
    for u in range(count):
        high, low = split(jnp.where(same_small, systems[u], 0.0))
        d_scr[u] = dot(high, pick) + dot(low, pick)
    for u in range(count):
        rows = [unit[0]]
        for i in range(1, SMALL):
            coef = d_scr[u, pl.ds(i, blocks, stride=SMALL), :]
            value = unit[i]
            for j in range(i):
                value = value - coef[:, j : j + 1] * rows[j]
            rows.append(value)
        for i in range(SMALL):
            t_scr[u, pl.ds(i, blocks, stride=SMALL), :] = rows[i]
    found = [t_scr[u] for u in range(count)]
    size = SMALL
    while 2 * size < tokens:
        mask = jnp.logical_and((row // (2 * size)) == (col // (2 * size)), (row // size) != (col // size))
        parts = [split(t) for t in found]
        inner = [dot3(split(jnp.where(mask, systems[u], 0.0)), parts[u]) for u in range(count)]
        found = [found[u] - dot3(parts[u], split(inner[u])) for u in range(count)]
        size *= 2
    upper = [split(t[:size, :size]) for t in found]
    lower = [split(t[size:, size:]) for t in found]
    inner = [dot3(split(systems[u][size:, :size]), upper[u]) for u in range(count)]
    corner = [dot3(lower[u], split(inner[u])) for u in range(count)]
    return [
        jnp.concatenate(
            [found[u][:size], jnp.concatenate([-corner[u], found[u][size:, size:]], axis=1)], axis=0
        )
        for u in range(count)
    ]


def norms(key, eye):
    gram = dot(key, key, NT)
    on_diag = jnp.where(eye, gram, 0.0)
    return (
        gram,
        lax.rsqrt(jnp.sum(on_diag, axis=1, keepdims=True) + 1e-6),
        lax.rsqrt(jnp.sum(on_diag, axis=0, keepdims=True) + 1e-6),
    )


def pack_kernel(k_ref, v_ref, g_ref, b_ref, out_ref, g_scr, b_scr, e_scr, sems):
    size = out_ref.shape[0]
    tokens, heads = g_ref.shape[2], g_ref.shape[1]
    own = heads // size
    repeat = heads // (k_ref.shape[2] // DK)
    keys = max(1, own // repeat)
    copies = [
        pltpu.make_async_copy(g_ref, g_scr, sems.at[0]),
        pltpu.make_async_copy(b_ref, b_scr, sems.at[1]),
    ]
    for d in range(size):
        for i in range(keys):
            kh = d * own // repeat + i
            copies.append(
                pltpu.make_async_copy(
                    k_ref.at[0, :, kh * DK : (kh + 1) * DK],
                    out_ref.at[d, i * tokens : (i + 1) * tokens],
                    sems.at[len(copies)],
                )
            )
        for i in range(own):
            h = d * own + i
            copies.append(
                pltpu.make_async_copy(
                    v_ref.at[0, :, h * DV : (h + 1) * DV],
                    out_ref.at[d, (keys + i) * tokens : (keys + i + 1) * tokens],
                    sems.at[len(copies)],
                )
            )
    for copy in copies:
        copy.start()
    copies[0].wait()
    copies[1].wait()
    e_scr[...] = jnp.zeros_like(e_scr)
    for which, scr in ((0, g_scr), (1, b_scr)):
        rest = scr[0]
        for part in range(3):
            piece = rest.astype(BF16).astype(F32)
            rest = rest - piece
            for d in range(size):
                at = part * 2 * own + which * own
                e_scr[d, at : at + own] = piece[d * own : (d + 1) * own]
    for d in range(size):
        out_ref[d, (keys + own) * tokens :] = e_scr[d].astype(BF16)
    for copy in copies[2:]:
        copy.wait()


def local_kernel(
    q_ref, k_ref, v_ref, z_ref, g_ref, b_ref, gain_ref, query_ref, intra_ref, gate_ref, d_scr, t_scr
):
    tokens = k_ref.shape[1]
    heads = g_ref.shape[1]
    repeat = heads // (k_ref.shape[2] // DK)
    row, col = row_col(tokens)
    lower = row >= col
    eye = row == col
    gates = g_ref[0]
    betas = b_ref[0]
    tri = jnp.where(lower, 1.0, 0.0)
    cum_cols = dot(tri, gates, NT, HIGH)
    cum_rows = dot(gates, tri, NT, HIGH)
    beta_cols = dot(jnp.where(eye, 1.0, 0.0), betas, NT, HIGH)
    gain = gain_ref[0:1, :]
    key_side = [norms(k_ref[0, :, i * DK : (i + 1) * DK], eye) for i in range(heads // repeat)]
    systems = []
    for h in range(heads):
        gram, key_col, key_row = key_side[h // repeat]
        decay = jnp.exp(jnp.where(row > col, cum_cols[:, h : h + 1] - cum_rows[h : h + 1, :], -1e30))
        systems.append(decay * gram * (beta_cols[:, h : h + 1] * key_col) * key_row)
    found = inverses(systems, d_scr, t_scr)
    for h in range(heads):
        kh = h // repeat
        _, key_col, key_row = key_side[kh]
        key = k_ref[0, :, kh * DK : (kh + 1) * DK]
        if h % repeat == 0:
            query = q_ref[0, :, kh * DK : (kh + 1) * DK]
            queryf = query.astype(F32)
            query_col = lax.rsqrt(jnp.sum(queryf * queryf, axis=1, keepdims=True) + 1e-6) * DK**-0.5
            product = dot(query, key, NT) * query_col * key_row
        scaled = found[h] * betas[h : h + 1, :]
        update = dot(scaled.astype(BF16), v_ref[0, :, h * DV : (h + 1) * DV])
        erase = dot((scaled * (jnp.exp(cum_rows[h : h + 1, :]) * key_row)).astype(BF16), key)
        both = jnp.concatenate([erase, update], axis=1).astype(BF16)
        decay = jnp.exp(jnp.where(lower, cum_cols[:, h : h + 1] - cum_rows[h : h + 1, :], -1e30))
        mixed = dot((decay * product).astype(BF16), both)
        intra_ref[:, h * DV : (h + 1) * DV] = mixed[:, DK:]
        reach = jnp.exp(cum_cols[:, h : h + 1]) * query_col
        query_ref[:, h * DK : (h + 1) * DK] = (reach * queryf - mixed[:, :DK]).astype(BF16)
        z = z_ref[0, :, h * DV : (h + 1) * DV].astype(F32)
        gate_ref[:, h * DV : (h + 1) * DV] = gain * z / (1.0 + jnp.exp(-z))


def group_kernel(own, keys, x_ref, move_ref, add_ref, pair_ref, y_scr, d_scr, t_scr):
    shards = x_ref.shape[0]
    tokens = DK
    repeat = own // keys
    row, col = row_col(tokens)
    lower = row >= col
    eye = row == col
    base = (keys + own) * tokens
    take_row = lax.broadcasted_iota(jnp.int32, (8, EXTRA), 0)
    take_col = lax.broadcasted_iota(jnp.int32, (8, EXTRA), 1)
    take = jnp.where(
        jnp.logical_and(take_col % (2 * own) == take_row, take_col < 6 * own), 1.0, 0.0
    ).astype(BF16)
    plain = jnp.concatenate([dot(take, x_ref[j, base : base + EXTRA]) for j in range(shards)], axis=0)
    tri = jnp.where(lower, 1.0, 0.0)
    cum_cols = dot(tri, plain, NT, HIGH)
    cum_rows = dot(plain, tri, NT, HIGH)
    plain_cols = dot(jnp.where(eye, 1.0, 0.0), plain, NT, HIGH)

    @pl.when(pl.program_id(0) == 0)
    def _():
        for h in range(own):
            y_scr[h] = jnp.concatenate(
                [jnp.where(eye, 1.0, 0.0), jnp.zeros((tokens, DV), F32)], axis=1
            )

    units = [(j, h) for j in range(shards) for h in range(own)]
    key_side = {}
    for j in range(shards):
        for i in range(keys):
            key_side[j, i] = norms(x_ref[j, i * tokens : (i + 1) * tokens], eye)
    systems = []
    for j, h in units:
        gram, key_col, key_row = key_side[j, h // repeat]
        at = j * 8 + h
        decay = jnp.exp(jnp.where(row > col, cum_cols[:, at : at + 1] - cum_rows[at : at + 1, :], -1e30))
        systems.append(decay * gram * (plain_cols[:, at + own : at + own + 1] * key_col) * key_row)
    found = inverses(systems, d_scr, t_scr)
    moved = {}
    for u, (j, h) in enumerate(units):
        i = h // repeat
        _, key_col, key_row = key_side[j, i]
        at = j * 8 + h
        key = x_ref[j, i * tokens : (i + 1) * tokens]
        value = x_ref[j, (keys + h) * tokens : (keys + h + 1) * tokens]
        scaled = found[u] * plain[at + own : at + own + 1, :]
        high, low = split(scaled)
        update = dot(high, value) + dot(low, value)
        high, low = split(scaled * (jnp.exp(cum_rows[at : at + 1, :]) * key_row))
        erase = dot(high, key) + dot(low, key)
        last = cum_rows[at : at + 1, tokens - 1 :]
        weight = jnp.exp(last - cum_cols[:, at : at + 1]) * key_col
        high, low = split(jnp.concatenate([erase, update], axis=1) * weight)
        both = dot(key, high, TN) + dot(key, low, TN)
        moved[j, h] = (jnp.where(eye, jnp.exp(last), 0.0) - both[:, :DK], both[:, DK:])
    total = [y_scr[h] for h in range(own)]
    for j in range(shards):
        for h in range(own):
            move_ref[j, h] = total[h][:, :DK].astype(BF16)
            add_ref[j, h] = total[h][:, DK:]
            gone = dot3(split(moved[j, h][0]), split(total[h]))
            total[h] = jnp.concatenate([gone[:, :DK], gone[:, DK:] + moved[j, h][1]], axis=1)
    for h in range(own):
        y_scr[h] = total[h]
        pair_ref[h] = total[h].astype(BF16)


def spread(start, final, info_ref, move_ref, add_ref, out_ref):
    size, own = move_ref.shape[0], move_ref.shape[1]
    for h in range(own):
        at = start[h].astype(BF16)
        to = info_ref[1 + h]
        for j in range(size):
            entry = dot(move_ref[j, h], at) + add_ref[j, h]
            kept = jnp.where(to == j, final[h], jnp.zeros_like(final[h]))
            out_ref[j, h] = jnp.concatenate([entry, kept], axis=1).astype(BF16)


def pair_spread_kernel(info_ref, move_ref, add_ref, mine_ref, got_ref, out_ref):
    own = mine_ref.shape[0]
    late = info_ref[0] == 1
    start, final = [], []
    for h in range(own):
        mine, got = mine_ref[h], got_ref[h]
        first = jnp.where(late, got[:, DK:].astype(F32), mine[:, DK:].astype(F32))
        second = jnp.where(late, mine.astype(F32), got.astype(F32))
        final.append(dot(second[:, :DK].astype(BF16), first.astype(BF16)) + second[:, DK:])
        start.append(jnp.where(late, first, jnp.zeros_like(first)))
    spread(start, final, info_ref, move_ref, add_ref, out_ref)


def spread_kernel(info_ref, move_ref, add_ref, start_ref, final_ref, out_ref):
    own = start_ref.shape[0]
    start = [start_ref[h].astype(F32) for h in range(own)]
    final = [final_ref[h].astype(F32) for h in range(own)]
    spread(start, final, info_ref, move_ref, add_ref, out_ref)


def read_kernel(back_ref, query_ref, intra_ref, gate_ref, w_ref, out_ref, q_scr, i_scr, z_scr, w_scr, normed_scr, sems):
    heads = back_ref.shape[0]
    pieces, step = w_scr.shape[0], w_scr.shape[2]
    copies = [
        pltpu.make_async_copy(query_ref, q_scr, sems.at[0]),
        pltpu.make_async_copy(intra_ref, i_scr, sems.at[1]),
        pltpu.make_async_copy(gate_ref, z_scr, sems.at[2]),
    ] + [
        pltpu.make_async_copy(w_ref.at[:, c * step : (c + 1) * step], w_scr.at[c], sems.at[3 + c])
        for c in range(pieces)
    ]
    for copy in copies:
        copy.start()
    for copy in copies[:3]:
        copy.wait()
    for h in range(heads):
        cols = slice(h * DV, (h + 1) * DV)
        value = i_scr[:, cols] + dot(q_scr[:, cols], back_ref[h, :, :DV])
        scale = lax.rsqrt(jnp.mean(value * value, axis=1, keepdims=True) + 1e-6)
        normed_scr[:, cols] = (value * scale * z_scr[:, cols]).astype(BF16)
    for c in range(pieces):
        copies[3 + c].wait()
        out_ref[:, c * step : (c + 1) * step] = dot(normed_scr[...], w_scr[c]).astype(BF16)


def cost(micros):
    return pl.CostEstimate(flops=int(micros * 1.15e9), bytes_accessed=1 << 20, transcendentals=0)


def params(limit=VMEM_LIMIT):
    return pltpu.CompilerParams(vmem_limit_bytes=limit)


def pack(keys, values, log_decay, beta, size):
    tokens, heads, key_heads = keys.shape[1], log_decay.shape[1], keys.shape[2] // DK
    own = heads // size
    carried = max(1, own * key_heads // heads)
    rows = (carried + own) * tokens + EXTRA
    far = pl.BlockSpec(memory_space=pltpu.HBM)
    return pl.pallas_call(
        pack_kernel,
        in_specs=[far, far, far, far],
        out_shape=jax.ShapeDtypeStruct((size, rows, DK), BF16),
        scratch_shapes=[
            pltpu.VMEM(log_decay.shape, F32),
            pltpu.VMEM(beta.shape, F32),
            pltpu.VMEM((size, EXTRA, tokens), F32),
            pltpu.SemaphoreType.DMA((2 + size * (carried + own),)),
        ],
        compiler_params=params(VMEM_MOST),
        cost_estimate=cost(2),
        name="pack",
    )(keys, values, log_decay, beta)


def local_part(queries, keys, values, out_gate, log_decay, beta, gain):
    tokens, heads, key_heads = keys.shape[1], log_decay.shape[1], keys.shape[2] // DK
    step = min(8, heads)
    key_step = step * key_heads // heads
    wide = pl.BlockSpec((tokens, step * DV), lambda i: (0, i))
    narrow = pl.BlockSpec((1, tokens, key_step * DK), lambda i: (0, 0, i))
    broad = pl.BlockSpec((1, tokens, step * DV), lambda i: (0, 0, i))
    thin = pl.BlockSpec((1, step, tokens), lambda i: (0, i, 0))
    return pl.pallas_call(
        local_kernel,
        grid=(heads // step,),
        in_specs=[narrow, narrow, broad, broad, thin, thin, pl.BlockSpec((1, DV), lambda i: (0, 0))],
        out_specs=[wide, wide, wide],
        out_shape=[
            jax.ShapeDtypeStruct((tokens, heads * DK), BF16),
            jax.ShapeDtypeStruct((tokens, heads * DV), F32),
            jax.ShapeDtypeStruct((tokens, heads * DV), F32),
        ],
        scratch_shapes=[pltpu.VMEM((step, tokens, DK), F32), pltpu.VMEM((step, tokens, tokens), F32)],
        compiler_params=params(VMEM_MOST),
        cost_estimate=cost(12),
        name="local_part",
    )(queries, keys, values, out_gate, log_decay, beta, gain)


def group_maps(x, own, keys):
    size, rows = x.shape[0], x.shape[1]
    step = min(4, size)
    block = lambda i: (i, 0, 0, 0)
    return pl.pallas_call(
        lambda *refs: group_kernel(own, keys, *refs),
        grid=(size // step,),
        in_specs=[pl.BlockSpec((step, rows, DK), lambda i: (i, 0, 0))],
        out_specs=[
            pl.BlockSpec((step, own, DK, DK), block),
            pl.BlockSpec((step, own, DK, DV), block),
            pl.BlockSpec((own, DK, DK + DV), lambda i: (0, 0, 0)),
        ],
        out_shape=[
            jax.ShapeDtypeStruct((size, own, DK, DK), BF16),
            jax.ShapeDtypeStruct((size, own, DK, DV), F32),
            jax.ShapeDtypeStruct((own, DK, DK + DV), BF16),
        ],
        scratch_shapes=[
            pltpu.VMEM((own, DK, DK + DV), F32),
            pltpu.VMEM((step * own, DK, DK), F32),
            pltpu.VMEM((step * own, DK, DK), F32),
        ],
        compiler_params=params(),
        cost_estimate=cost(12),
        name="group_maps",
    )(x)


def spread_states(kernel, info, move, add, one, two):
    near = pl.BlockSpec(memory_space=pltpu.VMEM)
    size, own = move.shape[0], move.shape[1]
    return pl.pallas_call(
        kernel,
        in_specs=[pl.BlockSpec(memory_space=pltpu.SMEM), near, near, near, near],
        out_shape=jax.ShapeDtypeStruct((size, own, DK, 2 * DV), BF16),
        compiler_params=params(),
        cost_estimate=cost(2),
        name="spread_states",
    )(info, move, add, one, two)


def read_out(query, intra, gate, back, weight):
    tokens, width = query.shape
    columns = weight.shape[1]
    pieces = 8
    near = pl.BlockSpec(memory_space=pltpu.VMEM)
    far = pl.BlockSpec(memory_space=pltpu.HBM)
    return pl.pallas_call(
        read_kernel,
        in_specs=[near, far, far, far, far],
        out_shape=jax.ShapeDtypeStruct((tokens, columns), BF16),
        scratch_shapes=[
            pltpu.VMEM(query.shape, query.dtype),
            pltpu.VMEM(intra.shape, intra.dtype),
            pltpu.VMEM(gate.shape, gate.dtype),
            pltpu.VMEM((pieces, width, columns // pieces), BF16),
            pltpu.VMEM((tokens, width), BF16),
            pltpu.SemaphoreType.DMA((3 + pieces,)),
        ],
        compiler_params=params(VMEM_WIDE),
        cost_estimate=cost(4),
        name="read_out",
    )(back, query, intra, gate, weight)


def group_size(count, heads):
    return max(s for s in range(1, 9) if count % s == 0 and heads % s == 0)


def local(queries, keys, values, out_gate, log_decay, beta, norm_gain, out_weight, owner):
    tokens, heads = keys.shape[1], log_decay.shape[1]
    count = lax.axis_size("seq")
    me = lax.axis_index("seq")
    size = group_size(count, heads)
    groups = count // size
    own = heads // size
    carried = max(1, own * (keys.shape[2] // DK) // heads)
    members = [[g * size + i for i in range(size)] for g in range(groups)]

    def swap(x):
        return lax.all_to_all(x, "seq", 0, 0, axis_index_groups=members, tiled=True)

    def hop(x, source, target):
        return lax.ppermute(x, "seq", [(source * size + i, target * size + i) for i in range(size)])

    mine = lax.dynamic_slice_in_dim(owner[0], (me % size) * own, own) - (me // size) * size
    info = jnp.concatenate([(me // size)[None].astype(jnp.int32), mine])

    raw = swap(pack(keys, values, log_decay, beta, size))
    query, intra, gate = local_part(queries, keys, values, out_gate, log_decay, beta, norm_gain[None])
    raw, query, intra, gate = lax.optimization_barrier((raw, query, intra, gate))
    move, add, pair = group_maps(raw, own, carried)
    if groups == 2:
        got = lax.ppermute(pair, "seq", [(i, (i + size) % count) for i in range(count)])
        sent = spread_states(pair_spread_kernel, info, move, add, pair, got)
    else:
        start = jnp.zeros((own, DK, DV), F32)
        wide = pair.astype(F32)

        def leave(start):
            kept = jnp.einsum("hij,hjk->hik", wide[..., :DK], start, precision=HIGH)
            return kept + wide[..., DK:]

        for g in range(groups - 1):
            start = start + hop(leave(start).astype(BF16), g, g + 1).astype(F32)
        last = leave(start).astype(BF16)
        last = jnp.where(me // size == groups - 1, last, jnp.zeros_like(last))
        for g in range(groups - 1, 0, -1):
            last = last + hop(last, g, g - 1)
        sent = spread_states(spread_kernel, info, move, add, start, last)
    back = swap(sent)
    back = back.reshape(heads, DK, 2 * DV)
    decode_states = back[None, :, :, DV:].astype(F32)
    partial_value = read_out(query, intra, gate, back, out_weight)
    ranks = lax.axis_size("head")
    if ranks == 2:
        half = tokens // 2
        rank = lax.axis_index("head")
        keep = lax.dynamic_slice_in_dim(partial_value, rank * half, half)
        give = lax.dynamic_slice_in_dim(partial_value, (1 - rank) * half, half)
        got = lax.ppermute(give, "head", [(0, 1), (1, 0)])
        total = (keep.astype(F32) + got.astype(F32)).astype(BF16)
    else:
        total = lax.psum_scatter(partial_value, "head", scatter_dimension=0, tiled=True)
    return (total[:, None, :], decode_states)


def solution(mesh):
    placed = (
        P(None, "seq", "head"),
        P(None, "seq", "head"),
        P(None, "seq", "head"),
        P(None, "seq", "head"),
        P(None, "head", "seq"),
        P(None, "head", "seq"),
        P(),
        P("head", None),
        P(None, "head"),
    )
    return jax.shard_map(
        local,
        mesh=mesh,
        in_specs=placed,
        out_specs=(P(("seq", "head"), None, None), P("seq", "head", None, None)),
        check_vma=False,
    )
```

time: 80.4 us -> 71.8 us (0.89)
  Pallas kernels: 23.6 us -> 34.7 us
  starting transfers between devices: 22.2 us -> 12.9 us
  local copies, waits for them, and re-layouts: 4.87 us -> 0.04 us
  waiting for transfers between devices: 24.4 us -> 21 us
  other arithmetic: 3.89 us -> 2.01 us
    pallas_call x5, Pallas kernels: 23.6 us -> 34.7 us  [the longest x1 12.9 us: group_maps(): pl.pallas_call(lambda *refs: group_kernel(own, keys, *refs), grid=(size /...]
    all_to_all x3 -> x2, starting transfers between devices: 16.3 us -> 10.2 us  [swap(): return lax.all_to_all(x, 'seq', 0, 0, axis_index_groups=members, tiled=True)]
    unnamed x20 -> x6, local copies, waits for them, and re-layouts: 4.75 us -> 0.01 us
    ppermute x2 -> x1, starting transfers between devices: 5.78 us -> 2.66 us  [local(): lax.ppermute(pair, 'seq', [(i, (i + size) % count) for i in range(count)])]
    all_to_all x3 -> x2, waiting for transfers between devices: 16.8 us -> 14.7 us  [swap(): return lax.all_to_all(x, 'seq', 0, 0, axis_index_groups=members, tiled=True)]
    ppermute x2 -> x1, waiting for transfers between devices: 7.58 us -> 5.92 us  [local(): lax.ppermute(pair, 'seq', [(i, (i + size) % count) for i in range(count)])]
    convert_element_type x1, other arithmetic: 2.12 us -> 1.09 us  [local(): decode_states = back[None, :, :, DV:].astype(F32)]
    select_n x2 -> x0, other arithmetic: 0.91 us -> none  [the longest x1 0.91 us: local(): finals = swap(jnp.where(kept, last[None], jnp.zeros_like(last)[None]))]
  transfers between devices with their start and end apart: 6 -> 4, of which waited for: 4 -> 3; matrix products, arithmetic and copies ran while one was open for 4% -> 2% of each run, Pallas kernels for 10% -> 17%
where the time goes in v2:
time: 71.8 us; the launch traced here: 71.5 us
  Pallas kernels  34.7 us (48%)
  waiting for transfers between devices  21 us (29%)
  starting transfers between devices  12.9 us (18%)
  other arithmetic  2.01 us (3%)
    all_to_all x2, waiting for transfers between devices, swap(): return lax.all_to_all(x, 'seq', 0, 0, axis_index_groups=members, tiled=True)  14.7 us
    pallas_call x1, Pallas kernels, group_maps(): pl.pallas_call(lambda *refs: group_kernel(own, keys, *refs), grid=(size /...  12.9 us
    pallas_call x1, Pallas kernels, local_part(): pl.pallas_call(local_kernel, grid=(heads // step,), in_specs=[narrow, nar...  12.5 us
    all_to_all x2, starting transfers between devices, swap(): return lax.all_to_all(x, 'seq', 0, 0, axis_index_groups=members, tiled=True)  10.2 us
    ppermute x1, waiting for transfers between devices, local(): lax.ppermute(pair, 'seq', [(i, (i + size) % count) for i in range(count)])  5.92 us
    pallas_call x1, Pallas kernels, read_out(): pl.pallas_call(read_kernel, in_specs=[near, far, far, far, far], out_shap...  5.31 us
    ppermute x1, starting transfers between devices, local(): lax.ppermute(pair, 'seq', [(i, (i + size) % count) for i in range(count)])  2.66 us
    pallas_call x1, Pallas kernels, pack(): pl.pallas_call(pack_kernel, in_specs=[far, far, far, far], out_shape=jax....  2.25 us
  transfers between devices with their start and end apart: 4, of which 3 were waited for; matrix products, arithmetic and copies ran while one was open for 2% of the time, Pallas kernels for 17%

profile of v2, /device:TPU:0, one launch (start us, length us, event | category | flops | bytes accessed | tf_op | source)
XLA Modules:
  0.0 71.5 jit_solution(7413507219806588149)
XLA Ops:
  0.6 2.2 %pack.1 = bf16[8,400,128]{2,1,0:T(8,128)(2,1)} custom-call(bf16[1,128,1024]{2,1,0:T(8,128)(2,1)} %k_ref.3, bf16[1,128,2048]{2,1,0:T(8,128)(2,1)} %v_ref.3, f32[1,16,128]{2,1,0:T(8,128)} %g_ref.3, f32[1,16,128]{2,1,0:T(8,128)} %b_ref.3), custom_call_target="tpu_custom_call" | custom-call | flops 2300000000 | bytes 1048576 | tf_op jit(solution)/shard_map/pack/pallas_call | solution.py:329
  2.9 6.2 %all-to-all-start = ((bf16[8,400,128]{2,1,0:T(8,128)(2,1)}), bf16[8,400,128]{2,1,0:T(8,128)(2,1)S(1)}, u32[]{:S(2)}, u32[]{:S(2)}) async-start(bf16[8,400,128]{2,1,0:T(8,128)(2,1)} %pack.1), calls=%async_computation | async-start | bytes 1638400 | tf_op jit(solution)/shard_map/all_to_all | solution.py:451
  9.1 12.5 %local_part.1 = (bf16[128,2048]{1,0:T(8,128)(2,1)}, f32[128,2048]{1,0:T(8,128)}, f32[128,2048]{1,0:T(8,128)}) custom-call(bf16[1,128,1024]{2,1,0:T(8,128)(2,1)} %q_ref.1, bf16[1,128,1024]{2,1,0:T(8,128)(2,1)} %k_ref.3, bf16[1,128,2048]{2,1,0:T(8,128)(2,1)} %v_ref.3, bf16[1,128,2048]{2,1,0:T(8,128)(2,1)} %z_ref.1, f32[1,16,128]{2,1,0:T(8,128)} %g_ref.3, ...), custom_call_target="tpu_custom_call" | custom-call | flops 13799999488 | bytes 1048576 | tf_op jit(solution)/shard_map/local_part/pallas_call | solution.py:353
  21.5 0.0 all-to-all-done.refs_0_
  21.6 0.0 copy-start.2
  21.6 12.9 %group_maps.1 = (bf16[8,2,128,128]{3,2,1,0:T(8,128)(2,1)S(1)}, f32[8,2,128,128]{3,2,1,0:T(8,128)S(1)}, bf16[2,128,256]{2,1,0:T(8,128)(2,1)S(1)}) custom-call(bf16[8,400,128]{2,1,0:T(8,128)(2,1)S(1)} %all-to-all-done.refs_0_), custom_call_target="tpu_custom_call" | custom-call | flops 13799999488 | bytes 1048576 | tf_op jit(solution)/shard_map/group_maps/pallas_call | solution.py:374
  34.4 0.0 copy-start
  34.5 0.0 copy-start.1
  34.5 2.7 %collective-permute-start = (bf16[2,128,256]{2,1,0:T(8,128)(2,1)S(1)}, bf16[2,128,256]{2,1,0:T(8,128)(2,1)S(1)}, u32[]{:S(2)}, u32[]{:S(2)}) collective-permute-start(bf16[2,128,256]{2,1,0:T(8,128)(2,1)S(1)} %get-tuple-element.18.mine_ref), channel_id=1, source_target_pairs={{0,16},{2,18},{4,20},{6,22},{8,24},{10,26},{12,28},{14,30},{16,0},... | collective-permute-start | bytes 393224 | tf_op jit(solution)/shard_map/ppermute | solution.py:464
  37.1 0.0 copy-done.2
  37.1 0.1 fusion.3
  37.2 0.1 pad_add_fusion.info_ref
  37.3 5.9 %collective-permute-done.got_ref = bf16[2,128,256]{2,1,0:T(8,128)(2,1)S(1)} collective-permute-done((bf16[2,128,256]{2,1,0:T(8,128)(2,1)S(1)}, bf16[2,128,256]{2,1,0:T(8,128)(2,1)S(1)}, u32[]{:S(2)}, u32[]{:S(2)}) %collective-permute-start) | collective-permute-done | bytes 131104 | tf_op jit(solution)/shard_map/ppermute | solution.py:464
  43.2 1.8 %spread_states.1 = bf16[8,2,128,256]{3,2,1,0:T(8,128)(2,1)} custom-call(s32[3]{0:T(128)S(1)} %pad_add_fusion.info_ref, bf16[8,2,128,128]{3,2,1,0:T(8,128)(2,1)S(1)} %get-tuple-element.16.move_ref, f32[8,2,128,128]{3,2,1,0:T(8,128)S(1)} %get-tuple-element.17.add_ref, bf16[2,128,256]{2,1,0:T(8,128)(2,1)S(1)} %get-tuple-element.18.mine_ref, ...), custom_call_target="tpu_custom_call" | custom-call | flops 2300000000 | bytes 1048576 | tf_op jit(solution)/shard_map/spread_states/pallas_call | solution.py:402
  45.0 4.0 %all-to-all-start.1 = ((bf16[8,2,128,256]{3,2,1,0:T(8,128)(2,1)}), bf16[8,2,128,256]{3,2,1,0:T(8,128)(2,1)S(1)}, u32[]{:S(2)}, u32[]{:S(2)}) async-start(bf16[8,2,128,256]{3,2,1,0:T(8,128)(2,1)} %spread_states.1), calls=%async_computation.1 | async-start | bytes 2097152 | tf_op jit(solution)/shard_map/all_to_all | solution.py:451
  49.1 14.7 %all-to-all-done.1 = bf16[8,2,128,256]{3,2,1,0:T(8,128)(2,1)S(1)} async-done(((bf16[8,2,128,256]{3,2,1,0:T(8,128)(2,1)}), bf16[8,2,128,256]{3,2,1,0:T(8,128)(2,1)S(1)}, u32[]{:S(2)}, u32[]{:S(2)}) %all-to-all-start.1) | async-done | bytes 1048608 | tf_op jit(solution)/shard_map/all_to_all | solution.py:451
  63.7 0.0 copy-done
  63.7 0.0 copy-done.1
  63.7 5.3 %read_out.1 = bf16[128,2048]{1,0:T(8,128)(2,1)S(1)} custom-call(bf16[16,128,256]{2,1,0:T(8,128)(2,1)S(1)} %bitcast.12, bf16[128,2048]{1,0:T(8,128)(2,1)S(1)} %copy-done.1, f32[128,2048]{1,0:T(8,128)S(1)} %copy-done, f32[128,2048]{1,0:T(8,128)} %get-tuple-element.21.gate_ref, bf16[2048,2048]{1,0:T(8,128)(2,1)} %w_ref.1), custom_call_target="tpu_custom_call" | custom-call | flops 4600000000 | bytes 1048576 | tf_op jit(solution)/shard_map/read_out/pallas_call | solution.py:418
  69.1 0.1 collective-permute-start.1
  69.2 1.1 %fusion = f32[1,16,128,128]{3,2,1,0:T(8,128)} fusion(bf16[16,128,256]{2,1,0:T(8,128)(2,1)S(1)} %bitcast.13), kind=kLoop, calls=%fused_computation.1 | loop fusion | flops 262144 | bytes 1572864 | tf_op jit(solution)/shard_map/convert_element_type | solution.py:483
  70.3 0.4 collective-permute-done.1
  70.7 0.8 %fusion.1 = bf16[64,1,2048]{2,0,1:T(8,128)(2,1)} fusion(bf16[64,2048]{1,0:T(8,128)(2,1)S(1)} %collective-permute-done.1, bf16[128,2048]{1,0:T(8,128)(2,1)S(1)} %read_out.1, s32[]{:T(128)S(6)} %select_n.24), kind=kLoop, calls=%fused_computation.3 | loop fusion | flops 524288 | bytes 786436 | tf_op jit(solution)/shard_map/broadcast_in_dim | solution.py:495
  (1 shorter events, 0.0 us)
Async XLA Ops:
  2.9 18.7 %all-to-all-start = ((bf16[8,400,128]{2,1,0:T(8,128)(2,1)}), bf16[8,400,128]{2,1,0:T(8,128)(2,1)S(1)}, u32[]{:S(2)}, u32[]{:S(2)}) async-start(bf16[8,400,128]{2,1,0:T(8,128)(2,1)} %pack.1), calls=%async_computation | async-start | bytes 1638400 | tf_op jit(solution)/shard_map/all_to_all | solution.py:451
  21.6 15.6 %copy-start.2 = (s32[1,16]{1,0:T(1,128)S(1)}, s32[1,16]{1,0:T(1,128)}, u32[]{:S(2)}) copy-start(s32[1,16]{1,0:T(1,128)} %param.17) | copy-start | bytes 196
  34.4 29.3 %copy-start = (f32[128,2048]{1,0:T(8,128)S(1)}, f32[128,2048]{1,0:T(8,128)}, u32[]{:S(2)}) copy-start(f32[128,2048]{1,0:T(8,128)} %get-tuple-element.20.intra_ref) | copy-start | bytes 3145732
  34.5 29.3 %copy-start.1 = (bf16[128,2048]{1,0:T(8,128)(2,1)S(1)}, bf16[128,2048]{1,0:T(8,128)(2,1)}, u32[]{:S(2)}) copy-start(bf16[128,2048]{1,0:T(8,128)(2,1)} %get-tuple-element.19.query_ref) | copy-start | bytes 1572868
  34.5 8.7 %collective-permute-start = (bf16[2,128,256]{2,1,0:T(8,128)(2,1)S(1)}, bf16[2,128,256]{2,1,0:T(8,128)(2,1)S(1)}, u32[]{:S(2)}, u32[]{:S(2)}) collective-permute-start(bf16[2,128,256]{2,1,0:T(8,128)(2,1)S(1)} %get-tuple-element.18.mine_ref), channel_id=1, source_target_pairs={{0,16},{2,18},{4,20},{6,22},{8,24},{10,26},{12,28},{14,30},{16,0},... | collective-permute-start | bytes 393224 | tf_op jit(solution)/shard_map/ppermute | solution.py:464
  45.0 18.7 %all-to-all-start.1 = ((bf16[8,2,128,256]{3,2,1,0:T(8,128)(2,1)}), bf16[8,2,128,256]{3,2,1,0:T(8,128)(2,1)S(1)}, u32[]{:S(2)}, u32[]{:S(2)}) async-start(bf16[8,2,128,256]{3,2,1,0:T(8,128)(2,1)} %spread_states.1), calls=%async_computation.1 | async-start | bytes 2097152 | tf_op jit(solution)/shard_map/all_to_all | solution.py:451
  69.1 1.6 %collective-permute-start.1 = (bf16[64,2048]{1,0:T(8,128)(2,1)S(1)}, bf16[64,2048]{1,0:T(8,128)(2,1)S(1)}, u32[]{:S(2)}, u32[]{:S(2)}) collective-permute-start(bf16[64,2048]{1,0:T(8,128)(2,1)S(1)} %constant_dynamic-slice_fusion), channel_id=1, source_target_pairs={{0,1},{1,0},{2,3},{3,2},{4,5},{5,4},{6,7},{7,6},{8,9},{9,8},{10,11... | collective-permute-start | bytes 786440 | tf_op jit(solution)/shard_map/ppermute | solution.py:491

commit v3 on v2

--- a/solution.py
+++ b/solution.py
@@ -32,9 +32,7 @@
 
 
 def dot3(a, b):
-    width = b[0].shape[1]
-    both = dot(a[0], jnp.concatenate(b, axis=1))
-    return both[:, :width] + (both[:, width:] + dot(a[1], b[0]))
+    return dot(a[0], b[0]) + (dot(a[0], b[1]) + dot(a[1], b[0]))
 
 
 def row_col(size):
@@ -57,13 +55,11 @@
         high, low = split(jnp.where(same_small, systems[u], 0.0))
         d_scr[u] = dot(high, pick) + dot(low, pick)
     for u in range(count):
-        rows = [unit[0]]
-        for i in range(1, SMALL):
-            coef = d_scr[u, pl.ds(i, blocks, stride=SMALL), :]
-            value = unit[i]
-            for j in range(i):
-                value = value - coef[:, j : j + 1] * rows[j]
-            rows.append(value)
+        rows = list(unit)
+        coef = [d_scr[u, pl.ds(i, blocks, stride=SMALL), :] for i in range(SMALL)]
+        for j in range(SMALL - 1):
+            for i in range(j + 1, SMALL):
+                rows[i] = rows[i] - coef[i][:, j : j + 1] * rows[j]
         for i in range(SMALL):
             t_scr[u, pl.ds(i, blocks, stride=SMALL), :] = rows[i]
     found = [t_scr[u] for u in range(count)]
@@ -369,7 +365,7 @@
 
 def group_maps(x, own, keys):
     size, rows = x.shape[0], x.shape[1]
-    step = min(4, size)
+    step = size
     block = lambda i: (i, 0, 0, 0)
     return pl.pallas_call(
         lambda *refs: group_kernel(own, keys, *refs),

time: 71.8 us -> 68.1 us (0.948)
  Pallas kernels: 34.7 us -> 31 us
    pallas_call x1, Pallas kernels: 12.9 us -> 10.1 us  [group_maps(): pl.pallas_call(lambda *refs: group_kernel(own, keys, *refs), grid=(size /...]
    pallas_call x1, Pallas kernels: 12.5 us -> 11.5 us  [local_part(): pl.pallas_call(local_kernel, grid=(heads // step,), in_specs=[narrow, nar...]
  transfers between devices with their start and end apart: 4 -> 4, of which waited for: 3 -> 4; matrix products, arithmetic and copies ran while one was open for 2% -> 2% of each run, Pallas kernels for 17% -> 17%
where the time goes in v3:
time: 68.1 us; the launch traced here: 67.7 us
  Pallas kernels  31 us (46%)
  waiting for transfers between devices  21.3 us (31%)
  starting transfers between devices  12.7 us (19%)
  other arithmetic  2.01 us (3%)
  between operations  0.71 us (1%)
    all_to_all x2, waiting for transfers between devices, swap(): return lax.all_to_all(x, 'seq', 0, 0, axis_index_groups=members, tiled=True)  15.2 us
    pallas_call x1, Pallas kernels, local_part(): pl.pallas_call(local_kernel, grid=(heads // step,), in_specs=[narrow, nar...  11.5 us
    pallas_call x1, Pallas kernels, group_maps(): pl.pallas_call(lambda *refs: group_kernel(own, keys, *refs), grid=(size /...  10.1 us
    all_to_all x2, starting transfers between devices, swap(): return lax.all_to_all(x, 'seq', 0, 0, axis_index_groups=members, tiled=True)  9.97 us
    ppermute x1, waiting for transfers between devices, local(): lax.ppermute(pair, 'seq', [(i, (i + size) % count) for i in range(count)])  5.61 us
    pallas_call x1, Pallas kernels, read_out(): pl.pallas_call(read_kernel, in_specs=[near, far, far, far, far], out_shap...  5.32 us
    ppermute x1, starting transfers between devices, local(): lax.ppermute(pair, 'seq', [(i, (i + size) % count) for i in range(count)])  2.66 us
    pallas_call x1, Pallas kernels, pack(): pl.pallas_call(pack_kernel, in_specs=[far, far, far, far], out_shape=jax....  2.25 us
  transfers between devices with their start and end apart: 4, of which 4 were waited for; matrix products, arithmetic and copies ran while one was open for 2% of the time, Pallas kernels for 17%

profile of v3, /device:TPU:0, one launch (start us, length us, event | category | flops | bytes accessed | tf_op | source)
XLA Modules:
  0.0 67.7 jit_solution(14487027357993636531)
XLA Ops:
  0.6 2.2 %pack.1 = bf16[8,400,128]{2,1,0:T(8,128)(2,1)} custom-call(bf16[1,128,1024]{2,1,0:T(8,128)(2,1)} %k_ref.3, bf16[1,128,2048]{2,1,0:T(8,128)(2,1)} %v_ref.3, f32[1,16,128]{2,1,0:T(8,128)} %g_ref.3, f32[1,16,128]{2,1,0:T(8,128)} %b_ref.3), custom_call_target="tpu_custom_call" | custom-call | flops 2300000000 | bytes 1048576 | tf_op jit(solution)/shard_map/pack/pallas_call | solution.py:325
  2.9 6.2 %all-to-all-start = ((bf16[8,400,128]{2,1,0:T(8,128)(2,1)}), bf16[8,400,128]{2,1,0:T(8,128)(2,1)S(1)}, u32[]{:S(2)}, u32[]{:S(2)}) async-start(bf16[8,400,128]{2,1,0:T(8,128)(2,1)} %pack.1), calls=%async_computation | async-start | bytes 1638400 | tf_op jit(solution)/shard_map/all_to_all | solution.py:447
  9.1 11.5 %local_part.1 = (bf16[128,2048]{1,0:T(8,128)(2,1)}, f32[128,2048]{1,0:T(8,128)}, f32[128,2048]{1,0:T(8,128)}) custom-call(bf16[1,128,1024]{2,1,0:T(8,128)(2,1)} %q_ref.1, bf16[1,128,1024]{2,1,0:T(8,128)(2,1)} %k_ref.3, bf16[1,128,2048]{2,1,0:T(8,128)(2,1)} %v_ref.3, bf16[1,128,2048]{2,1,0:T(8,128)(2,1)} %z_ref.1, f32[1,16,128]{2,1,0:T(8,128)} %g_ref.3, ...), custom_call_target="tpu_custom_call" | custom-call | flops 13799999488 | bytes 1048576 | tf_op jit(solution)/shard_map/local_part/pallas_call | solution.py:349
  20.6 0.6 all-to-all-done.refs_0_
  21.2 0.0 copy-start.2
  21.2 10.1 %group_maps.1 = (bf16[8,2,128,128]{3,2,1,0:T(8,128)(2,1)S(1)}, f32[8,2,128,128]{3,2,1,0:T(8,128)S(1)}, bf16[2,128,256]{2,1,0:T(8,128)(2,1)S(1)}) custom-call(bf16[8,400,128]{2,1,0:T(8,128)(2,1)S(1)} %all-to-all-done.refs_0_), custom_call_target="tpu_custom_call" | custom-call | flops 13799999488 | bytes 1048576 | tf_op jit(solution)/shard_map/group_maps/pallas_call | solution.py:370
  31.3 0.0 copy-start
  31.3 0.0 copy-start.1
  31.3 2.7 %collective-permute-start = (bf16[2,128,256]{2,1,0:T(8,128)(2,1)S(1)}, bf16[2,128,256]{2,1,0:T(8,128)(2,1)S(1)}, u32[]{:S(2)}, u32[]{:S(2)}) collective-permute-start(bf16[2,128,256]{2,1,0:T(8,128)(2,1)S(1)} %get-tuple-element.18.mine_ref), channel_id=1, source_target_pairs={{0,16},{2,18},{4,20},{6,22},{8,24},{10,26},{12,28},{14,30},{16,0},... | collective-permute-start | bytes 393224 | tf_op jit(solution)/shard_map/ppermute | solution.py:460
  34.0 0.0 copy-done.2
  34.0 0.1 fusion.3
  34.1 0.1 pad_add_fusion.info_ref
  34.1 5.6 %collective-permute-done.got_ref = bf16[2,128,256]{2,1,0:T(8,128)(2,1)S(1)} collective-permute-done((bf16[2,128,256]{2,1,0:T(8,128)(2,1)S(1)}, bf16[2,128,256]{2,1,0:T(8,128)(2,1)S(1)}, u32[]{:S(2)}, u32[]{:S(2)}) %collective-permute-start) | collective-permute-done | bytes 131104 | tf_op jit(solution)/shard_map/ppermute | solution.py:460
  39.7 1.8 %spread_states.1 = bf16[8,2,128,256]{3,2,1,0:T(8,128)(2,1)} custom-call(s32[3]{0:T(128)S(1)} %pad_add_fusion.info_ref, bf16[8,2,128,128]{3,2,1,0:T(8,128)(2,1)S(1)} %get-tuple-element.16.move_ref, f32[8,2,128,128]{3,2,1,0:T(8,128)S(1)} %get-tuple-element.17.add_ref, bf16[2,128,256]{2,1,0:T(8,128)(2,1)S(1)} %get-tuple-element.18.mine_ref, ...), custom_call_target="tpu_custom_call" | custom-call | flops 2300000000 | bytes 1048576 | tf_op jit(solution)/shard_map/spread_states/pallas_call | solution.py:398
  41.6 3.8 %all-to-all-start.1 = ((bf16[8,2,128,256]{3,2,1,0:T(8,128)(2,1)}), bf16[8,2,128,256]{3,2,1,0:T(8,128)(2,1)S(1)}, u32[]{:S(2)}, u32[]{:S(2)}) async-start(bf16[8,2,128,256]{3,2,1,0:T(8,128)(2,1)} %spread_states.1), calls=%async_computation.1 | async-start | bytes 2097152 | tf_op jit(solution)/shard_map/all_to_all | solution.py:447
  45.4 14.6 %all-to-all-done.1 = bf16[8,2,128,256]{3,2,1,0:T(8,128)(2,1)S(1)} async-done(((bf16[8,2,128,256]{3,2,1,0:T(8,128)(2,1)}), bf16[8,2,128,256]{3,2,1,0:T(8,128)(2,1)S(1)}, u32[]{:S(2)}, u32[]{:S(2)}) %all-to-all-start.1) | async-done | bytes 1048608 | tf_op jit(solution)/shard_map/all_to_all | solution.py:447
  60.0 0.0 copy-done
  60.0 0.0 copy-done.1
  60.0 5.3 %read_out.1 = bf16[128,2048]{1,0:T(8,128)(2,1)S(1)} custom-call(bf16[16,128,256]{2,1,0:T(8,128)(2,1)S(1)} %bitcast.12, bf16[128,2048]{1,0:T(8,128)(2,1)S(1)} %copy-done.1, f32[128,2048]{1,0:T(8,128)S(1)} %copy-done, f32[128,2048]{1,0:T(8,128)} %get-tuple-element.21.gate_ref, bf16[2048,2048]{1,0:T(8,128)(2,1)} %w_ref.1), custom_call_target="tpu_custom_call" | custom-call | flops 4600000000 | bytes 1048576 | tf_op jit(solution)/shard_map/read_out/pallas_call | solution.py:414
  65.4 0.1 collective-permute-start.1
  65.5 1.1 %fusion = f32[1,16,128,128]{3,2,1,0:T(8,128)} fusion(bf16[16,128,256]{2,1,0:T(8,128)(2,1)S(1)} %bitcast.13), kind=kLoop, calls=%fused_computation.1 | loop fusion | flops 262144 | bytes 1572864 | tf_op jit(solution)/shard_map/convert_element_type | solution.py:479
  66.5 0.4 collective-permute-done.1
  67.0 0.8 %fusion.1 = bf16[64,1,2048]{2,0,1:T(8,128)(2,1)} fusion(bf16[64,2048]{1,0:T(8,128)(2,1)S(1)} %collective-permute-done.1, bf16[128,2048]{1,0:T(8,128)(2,1)S(1)} %read_out.1, s32[]{:T(128)S(6)} %select_n.24), kind=kLoop, calls=%fused_computation.3 | loop fusion | flops 524288 | bytes 786436 | tf_op jit(solution)/shard_map/broadcast_in_dim | solution.py:491
  (1 shorter events, 0.0 us)
Async XLA Ops:
  2.9 18.3 %all-to-all-start = ((bf16[8,400,128]{2,1,0:T(8,128)(2,1)}), bf16[8,400,128]{2,1,0:T(8,128)(2,1)S(1)}, u32[]{:S(2)}, u32[]{:S(2)}) async-start(bf16[8,400,128]{2,1,0:T(8,128)(2,1)} %pack.1), calls=%async_computation | async-start | bytes 1638400 | tf_op jit(solution)/shard_map/all_to_all | solution.py:447
  21.2 12.8 %copy-start.2 = (s32[1,16]{1,0:T(1,128)S(1)}, s32[1,16]{1,0:T(1,128)}, u32[]{:S(2)}) copy-start(s32[1,16]{1,0:T(1,128)} %param.17) | copy-start | bytes 196
  31.3 28.7 %copy-start = (f32[128,2048]{1,0:T(8,128)S(1)}, f32[128,2048]{1,0:T(8,128)}, u32[]{:S(2)}) copy-start(f32[128,2048]{1,0:T(8,128)} %get-tuple-element.20.intra_ref) | copy-start | bytes 3145732
  31.3 28.7 %copy-start.1 = (bf16[128,2048]{1,0:T(8,128)(2,1)S(1)}, bf16[128,2048]{1,0:T(8,128)(2,1)}, u32[]{:S(2)}) copy-start(bf16[128,2048]{1,0:T(8,128)(2,1)} %get-tuple-element.19.query_ref) | copy-start | bytes 1572868
  31.3 8.4 %collective-permute-start = (bf16[2,128,256]{2,1,0:T(8,128)(2,1)S(1)}, bf16[2,128,256]{2,1,0:T(8,128)(2,1)S(1)}, u32[]{:S(2)}, u32[]{:S(2)}) collective-permute-start(bf16[2,128,256]{2,1,0:T(8,128)(2,1)S(1)} %get-tuple-element.18.mine_ref), channel_id=1, source_target_pairs={{0,16},{2,18},{4,20},{6,22},{8,24},{10,26},{12,28},{14,30},{16,0},... | collective-permute-start | bytes 393224 | tf_op jit(solution)/shard_map/ppermute | solution.py:460
  41.6 18.4 %all-to-all-start.1 = ((bf16[8,2,128,256]{3,2,1,0:T(8,128)(2,1)}), bf16[8,2,128,256]{3,2,1,0:T(8,128)(2,1)S(1)}, u32[]{:S(2)}, u32[]{:S(2)}) async-start(bf16[8,2,128,256]{3,2,1,0:T(8,128)(2,1)} %spread_states.1), calls=%async_computation.1 | async-start | bytes 2097152 | tf_op jit(solution)/shard_map/all_to_all | solution.py:447
  65.4 1.6 %collective-permute-start.1 = (bf16[64,2048]{1,0:T(8,128)(2,1)S(1)}, bf16[64,2048]{1,0:T(8,128)(2,1)S(1)}, u32[]{:S(2)}, u32[]{:S(2)}) collective-permute-start(bf16[64,2048]{1,0:T(8,128)(2,1)S(1)} %constant_dynamic-slice_fusion), channel_id=1, source_target_pairs={{0,1},{1,0},{2,3},{3,2},{4,5},{5,4},{6,7},{7,6},{8,9},{9,8},{10,11... | collective-permute-start | bytes 786440 | tf_op jit(solution)/shard_map/ppermute | solution.py:487

commit v4 on v3

--- a/solution.py
+++ b/solution.py
@@ -185,7 +185,7 @@
         gate_ref[:, h * DV : (h + 1) * DV] = gain * z / (1.0 + jnp.exp(-z))
 
 
-def group_kernel(own, keys, x_ref, move_ref, add_ref, pair_ref, y_scr, d_scr, t_scr):
+def group_kernel(own, keys, x_ref, move_ref, add_ref, pair_ref, d_scr, t_scr):
     shards = x_ref.shape[0]
     tokens = DK
     repeat = own // keys
@@ -204,13 +204,6 @@
     cum_rows = dot(plain, tri, NT, HIGH)
     plain_cols = dot(jnp.where(eye, 1.0, 0.0), plain, NT, HIGH)
 
-    @pl.when(pl.program_id(0) == 0)
-    def _():
-        for h in range(own):
-            y_scr[h] = jnp.concatenate(
-                [jnp.where(eye, 1.0, 0.0), jnp.zeros((tokens, DV), F32)], axis=1
-            )
-
     units = [(j, h) for j in range(shards) for h in range(own)]
     key_side = {}
     for j in range(shards):
@@ -223,24 +216,29 @@
         decay = jnp.exp(jnp.where(row > col, cum_cols[:, at : at + 1] - cum_rows[at : at + 1, :], -1e30))
         systems.append(decay * gram * (plain_cols[:, at + own : at + own + 1] * key_col) * key_row)
     found = inverses(systems, d_scr, t_scr)
-    moved = {}
-    for u, (j, h) in enumerate(units):
-        i = h // repeat
-        _, key_col, key_row = key_side[j, i]
-        at = j * 8 + h
-        key = x_ref[j, i * tokens : (i + 1) * tokens]
-        value = x_ref[j, (keys + h) * tokens : (keys + h + 1) * tokens]
-        scaled = found[u] * plain[at + own : at + own + 1, :]
-        high, low = split(scaled)
-        update = dot(high, value) + dot(low, value)
-        high, low = split(scaled * (jnp.exp(cum_rows[at : at + 1, :]) * key_row))
-        erase = dot(high, key) + dot(low, key)
-        last = cum_rows[at : at + 1, tokens - 1 :]
-        weight = jnp.exp(last - cum_cols[:, at : at + 1]) * key_col
-        high, low = split(jnp.concatenate([erase, update], axis=1) * weight)
-        both = dot(key, high, TN) + dot(key, low, TN)
-        moved[j, h] = (jnp.where(eye, jnp.exp(last), 0.0) - both[:, :DK], both[:, DK:])
-    total = [y_scr[h] for h in range(own)]
+    rows_at = [j * 8 + h for j, h in units]
+    keys_of = [x_ref[j, (h // repeat) * tokens : (h // repeat + 1) * tokens] for j, h in units]
+    values_of = [x_ref[j, (keys + h) * tokens : (keys + h + 1) * tokens] for j, h in units]
+    sides = [key_side[j, h // repeat] for j, h in units]
+    count = range(len(units))
+    scaled = [found[u] * plain[rows_at[u] + own : rows_at[u] + own + 1, :] for u in count]
+    forward = [jnp.exp(cum_rows[at : at + 1, :]) * side[2] for at, side in zip(rows_at, sides)]
+    left = [split(scaled[u]) for u in count]
+    right = [split(scaled[u] * forward[u]) for u in count]
+    update = [dot(left[u][0], values_of[u]) + dot(left[u][1], values_of[u]) for u in count]
+    erase = [dot(right[u][0], keys_of[u]) + dot(right[u][1], keys_of[u]) for u in count]
+    lasts = [cum_rows[at : at + 1, tokens - 1 :] for at in rows_at]
+    weights = [
+        jnp.exp(lasts[u] - cum_cols[:, rows_at[u] : rows_at[u] + 1]) * sides[u][1] for u in count
+    ]
+    solved = [split(jnp.concatenate([erase[u], update[u]], axis=1) * weights[u]) for u in count]
+    both = [dot(keys_of[u], solved[u][0], TN) + dot(keys_of[u], solved[u][1], TN) for u in count]
+    moved = {
+        units[u]: (jnp.where(eye, jnp.exp(lasts[u]), 0.0) - both[u][:, :DK], both[u][:, DK:])
+        for u in count
+    }
+    start = jnp.concatenate([jnp.where(eye, 1.0, 0.0), jnp.zeros((tokens, DV), F32)], axis=1)
+    total = [start for _ in range(own)]
     for j in range(shards):
         for h in range(own):
             move_ref[j, h] = total[h][:, :DK].astype(BF16)
@@ -248,7 +246,6 @@
             gone = dot3(split(moved[j, h][0]), split(total[h]))
             total[h] = jnp.concatenate([gone[:, :DK], gone[:, DK:] + moved[j, h][1]], axis=1)
     for h in range(own):
-        y_scr[h] = total[h]
         pair_ref[h] = total[h].astype(BF16)
 
 
@@ -364,27 +361,20 @@
 
 
 def group_maps(x, own, keys):
-    size, rows = x.shape[0], x.shape[1]
-    step = size
-    block = lambda i: (i, 0, 0, 0)
+    size = x.shape[0]
+    near = pl.BlockSpec(memory_space=pltpu.VMEM)
     return pl.pallas_call(
         lambda *refs: group_kernel(own, keys, *refs),
-        grid=(size // step,),
-        in_specs=[pl.BlockSpec((step, rows, DK), lambda i: (i, 0, 0))],
-        out_specs=[
-            pl.BlockSpec((step, own, DK, DK), block),
-            pl.BlockSpec((step, own, DK, DV), block),
-            pl.BlockSpec((own, DK, DK + DV), lambda i: (0, 0, 0)),
-        ],
+        in_specs=[near],
+        out_specs=[near, near, near],
         out_shape=[
             jax.ShapeDtypeStruct((size, own, DK, DK), BF16),
             jax.ShapeDtypeStruct((size, own, DK, DV), F32),
             jax.ShapeDtypeStruct((own, DK, DK + DV), BF16),
         ],
         scratch_shapes=[
-            pltpu.VMEM((own, DK, DK + DV), F32),
-            pltpu.VMEM((step * own, DK, DK), F32),
-            pltpu.VMEM((step * own, DK, DK), F32),
+            pltpu.VMEM((size * own, DK, DK), F32),
+            pltpu.VMEM((size * own, DK, DK), F32),
         ],
         compiler_params=params(),
         cost_estimate=cost(12),

time: 68.1 us -> 67.9 us (level)
  no operation moved by 1% of the time
where the time goes in v4:
time: 67.9 us; the launch traced here: 67.5 us
  Pallas kernels  30.8 us (45%)
  waiting for transfers between devices  21.3 us (31%)
  starting transfers between devices  12.7 us (19%)
  other arithmetic  2.01 us (3%)
  between operations  0.69 us (1%)
    all_to_all x2, waiting for transfers between devices, swap(): return lax.all_to_all(x, 'seq', 0, 0, axis_index_groups=members, tiled=True)  15.3 us
    pallas_call x1, Pallas kernels, local_part(): pl.pallas_call(local_kernel, grid=(heads // step,), in_specs=[narrow, nar...  11.5 us
    all_to_all x2, starting transfers between devices, swap(): return lax.all_to_all(x, 'seq', 0, 0, axis_index_groups=members, tiled=True)  9.95 us
    pallas_call x1, Pallas kernels, group_maps(): pl.pallas_call(lambda *refs: group_kernel(own, keys, *refs), in_specs=[ne...  9.89 us
    ppermute x1, waiting for transfers between devices, local(): lax.ppermute(pair, 'seq', [(i, (i + size) % count) for i in range(count)])  5.61 us
    pallas_call x1, Pallas kernels, read_out(): pl.pallas_call(read_kernel, in_specs=[near, far, far, far, far], out_shap...  5.32 us
    ppermute x1, starting transfers between devices, local(): lax.ppermute(pair, 'seq', [(i, (i + size) % count) for i in range(count)])  2.66 us
    pallas_call x1, Pallas kernels, pack(): pl.pallas_call(pack_kernel, in_specs=[far, far, far, far], out_shape=jax....  2.25 us
  transfers between devices with their start and end apart: 4, of which 4 were waited for; matrix products, arithmetic and copies ran while one was open for 2% of the time, Pallas kernels for 17%

profile of v4, /device:TPU:0, one launch (start us, length us, event | category | flops | bytes accessed | tf_op | source)
XLA Modules:
  0.0 67.5 jit_solution(17099718703530101537)
XLA Ops:
  0.6 2.2 %pack.1 = bf16[8,400,128]{2,1,0:T(8,128)(2,1)} custom-call(bf16[1,128,1024]{2,1,0:T(8,128)(2,1)} %k_ref.3, bf16[1,128,2048]{2,1,0:T(8,128)(2,1)} %v_ref.3, f32[1,16,128]{2,1,0:T(8,128)} %g_ref.3, f32[1,16,128]{2,1,0:T(8,128)} %b_ref.3), custom_call_target="tpu_custom_call" | custom-call | flops 2300000000 | bytes 1048576 | tf_op jit(solution)/shard_map/pack/pallas_call | solution.py:322
  2.9 6.2 %all-to-all-start = ((bf16[8,400,128]{2,1,0:T(8,128)(2,1)}), bf16[8,400,128]{2,1,0:T(8,128)(2,1)S(1)}, u32[]{:S(2)}, u32[]{:S(2)}) async-start(bf16[8,400,128]{2,1,0:T(8,128)(2,1)} %pack.1), calls=%async_computation | async-start | bytes 1638400 | tf_op jit(solution)/shard_map/all_to_all | solution.py:437
  9.1 11.5 %local_part.1 = (bf16[128,2048]{1,0:T(8,128)(2,1)}, f32[128,2048]{1,0:T(8,128)}, f32[128,2048]{1,0:T(8,128)}) custom-call(bf16[1,128,1024]{2,1,0:T(8,128)(2,1)} %q_ref.1, bf16[1,128,1024]{2,1,0:T(8,128)(2,1)} %k_ref.3, bf16[1,128,2048]{2,1,0:T(8,128)(2,1)} %v_ref.3, bf16[1,128,2048]{2,1,0:T(8,128)(2,1)} %z_ref.1, f32[1,16,128]{2,1,0:T(8,128)} %g_ref.3, ...), custom_call_target="tpu_custom_call" | custom-call | flops 13799999488 | bytes 1048576 | tf_op jit(solution)/shard_map/local_part/pallas_call | solution.py:346
  20.6 0.6 all-to-all-done.refs_0_
  21.2 0.0 copy-start.2
  21.2 9.9 %group_maps.1 = (bf16[8,2,128,128]{3,2,1,0:T(8,128)(2,1)S(1)}, f32[8,2,128,128]{3,2,1,0:T(8,128)S(1)}, bf16[2,128,256]{2,1,0:T(8,128)(2,1)S(1)}) custom-call(bf16[8,400,128]{2,1,0:T(8,128)(2,1)S(1)} %all-to-all-done.refs_0_), custom_call_target="tpu_custom_call" | custom-call | flops 13799999488 | bytes 1048576 | tf_op jit(solution)/shard_map/group_maps/pallas_call | solution.py:366
  31.1 0.0 copy-start
  31.1 0.0 copy-start.1
  31.1 2.7 %collective-permute-start = (bf16[2,128,256]{2,1,0:T(8,128)(2,1)S(1)}, bf16[2,128,256]{2,1,0:T(8,128)(2,1)S(1)}, u32[]{:S(2)}, u32[]{:S(2)}) collective-permute-start(bf16[2,128,256]{2,1,0:T(8,128)(2,1)S(1)} %get-tuple-element.18.mine_ref), channel_id=1, source_target_pairs={{0,16},{2,18},{4,20},{6,22},{8,24},{10,26},{12,28},{14,30},{16,0},... | collective-permute-start | bytes 393224 | tf_op jit(solution)/shard_map/ppermute | solution.py:450
  33.7 0.0 copy-done.2
  33.7 0.1 fusion.3
  33.8 0.1 pad_add_fusion.info_ref
  33.9 5.6 %collective-permute-done.got_ref = bf16[2,128,256]{2,1,0:T(8,128)(2,1)S(1)} collective-permute-done((bf16[2,128,256]{2,1,0:T(8,128)(2,1)S(1)}, bf16[2,128,256]{2,1,0:T(8,128)(2,1)S(1)}, u32[]{:S(2)}, u32[]{:S(2)}) %collective-permute-start) | collective-permute-done | bytes 131104 | tf_op jit(solution)/shard_map/ppermute | solution.py:450
  39.5 1.8 %spread_states.1 = bf16[8,2,128,256]{3,2,1,0:T(8,128)(2,1)} custom-call(s32[3]{0:T(128)S(1)} %pad_add_fusion.info_ref, bf16[8,2,128,128]{3,2,1,0:T(8,128)(2,1)S(1)} %get-tuple-element.16.move_ref, f32[8,2,128,128]{3,2,1,0:T(8,128)S(1)} %get-tuple-element.17.add_ref, bf16[2,128,256]{2,1,0:T(8,128)(2,1)S(1)} %get-tuple-element.18.mine_ref, ...), custom_call_target="tpu_custom_call" | custom-call | flops 2300000000 | bytes 1048576 | tf_op jit(solution)/shard_map/spread_states/pallas_call | solution.py:388
  41.3 3.8 %all-to-all-start.1 = ((bf16[8,2,128,256]{3,2,1,0:T(8,128)(2,1)}), bf16[8,2,128,256]{3,2,1,0:T(8,128)(2,1)S(1)}, u32[]{:S(2)}, u32[]{:S(2)}) async-start(bf16[8,2,128,256]{3,2,1,0:T(8,128)(2,1)} %spread_states.1), calls=%async_computation.1 | async-start | bytes 2097152 | tf_op jit(solution)/shard_map/all_to_all | solution.py:437
  45.1 14.7 %all-to-all-done.1 = bf16[8,2,128,256]{3,2,1,0:T(8,128)(2,1)S(1)} async-done(((bf16[8,2,128,256]{3,2,1,0:T(8,128)(2,1)}), bf16[8,2,128,256]{3,2,1,0:T(8,128)(2,1)S(1)}, u32[]{:S(2)}, u32[]{:S(2)}) %all-to-all-start.1) | async-done | bytes 1048608 | tf_op jit(solution)/shard_map/all_to_all | solution.py:437
  59.8 0.0 copy-done
  59.8 0.0 copy-done.1
  59.8 5.3 %read_out.1 = bf16[128,2048]{1,0:T(8,128)(2,1)S(1)} custom-call(bf16[16,128,256]{2,1,0:T(8,128)(2,1)S(1)} %bitcast.12, bf16[128,2048]{1,0:T(8,128)(2,1)S(1)} %copy-done.1, f32[128,2048]{1,0:T(8,128)S(1)} %copy-done, f32[128,2048]{1,0:T(8,128)} %get-tuple-element.21.gate_ref, bf16[2048,2048]{1,0:T(8,128)(2,1)} %w_ref.1), custom_call_target="tpu_custom_call" | custom-call | flops 4600000000 | bytes 1048576 | tf_op jit(solution)/shard_map/read_out/pallas_call | solution.py:404
  65.1 0.1 collective-permute-start.1
  65.2 1.1 %fusion = f32[1,16,128,128]{3,2,1,0:T(8,128)} fusion(bf16[16,128,256]{2,1,0:T(8,128)(2,1)S(1)} %bitcast.13), kind=kLoop, calls=%fused_computation.1 | loop fusion | flops 262144 | bytes 1572864 | tf_op jit(solution)/shard_map/convert_element_type | solution.py:469
  66.3 0.4 collective-permute-done.1
  66.7 0.8 %fusion.1 = bf16[64,1,2048]{2,0,1:T(8,128)(2,1)} fusion(bf16[64,2048]{1,0:T(8,128)(2,1)S(1)} %collective-permute-done.1, bf16[128,2048]{1,0:T(8,128)(2,1)S(1)} %read_out.1, s32[]{:T(128)S(6)} %select_n.24), kind=kLoop, calls=%fused_computation.3 | loop fusion | flops 524288 | bytes 786436 | tf_op jit(solution)/shard_map/broadcast_in_dim | solution.py:481
  (1 shorter events, 0.0 us)
Async XLA Ops:
  2.9 18.3 %all-to-all-start = ((bf16[8,400,128]{2,1,0:T(8,128)(2,1)}), bf16[8,400,128]{2,1,0:T(8,128)(2,1)S(1)}, u32[]{:S(2)}, u32[]{:S(2)}) async-start(bf16[8,400,128]{2,1,0:T(8,128)(2,1)} %pack.1), calls=%async_computation | async-start | bytes 1638400 | tf_op jit(solution)/shard_map/all_to_all | solution.py:437
  21.2 12.6 %copy-start.2 = (s32[1,16]{1,0:T(1,128)S(1)}, s32[1,16]{1,0:T(1,128)}, u32[]{:S(2)}) copy-start(s32[1,16]{1,0:T(1,128)} %param.17) | copy-start | bytes 196
  31.1 28.7 %copy-start = (f32[128,2048]{1,0:T(8,128)S(1)}, f32[128,2048]{1,0:T(8,128)}, u32[]{:S(2)}) copy-start(f32[128,2048]{1,0:T(8,128)} %get-tuple-element.20.intra_ref) | copy-start | bytes 3145732
  31.1 28.7 %copy-start.1 = (bf16[128,2048]{1,0:T(8,128)(2,1)S(1)}, bf16[128,2048]{1,0:T(8,128)(2,1)}, u32[]{:S(2)}) copy-start(bf16[128,2048]{1,0:T(8,128)(2,1)} %get-tuple-element.19.query_ref) | copy-start | bytes 1572868
  31.1 8.4 %collective-permute-start = (bf16[2,128,256]{2,1,0:T(8,128)(2,1)S(1)}, bf16[2,128,256]{2,1,0:T(8,128)(2,1)S(1)}, u32[]{:S(2)}, u32[]{:S(2)}) collective-permute-start(bf16[2,128,256]{2,1,0:T(8,128)(2,1)S(1)} %get-tuple-element.18.mine_ref), channel_id=1, source_target_pairs={{0,16},{2,18},{4,20},{6,22},{8,24},{10,26},{12,28},{14,30},{16,0},... | collective-permute-start | bytes 393224 | tf_op jit(solution)/shard_map/ppermute | solution.py:450
  41.3 18.4 %all-to-all-start.1 = ((bf16[8,2,128,256]{3,2,1,0:T(8,128)(2,1)}), bf16[8,2,128,256]{3,2,1,0:T(8,128)(2,1)S(1)}, u32[]{:S(2)}, u32[]{:S(2)}) async-start(bf16[8,2,128,256]{3,2,1,0:T(8,128)(2,1)} %spread_states.1), calls=%async_computation.1 | async-start | bytes 2097152 | tf_op jit(solution)/shard_map/all_to_all | solution.py:437
  65.1 1.6 %collective-permute-start.1 = (bf16[64,2048]{1,0:T(8,128)(2,1)S(1)}, bf16[64,2048]{1,0:T(8,128)(2,1)S(1)}, u32[]{:S(2)}, u32[]{:S(2)}) collective-permute-start(bf16[64,2048]{1,0:T(8,128)(2,1)S(1)} %constant_dynamic-slice_fusion), channel_id=1, source_target_pairs={{0,1},{1,0},{2,3},{3,2},{4,5},{5,4},{6,7},{7,6},{8,9},{9,8},{10,11... | collective-permute-start | bytes 786440 | tf_op jit(solution)/shard_map/ppermute | solution.py:477

commit v5 on v4

--- a/solution.py
+++ b/solution.py
@@ -398,7 +398,7 @@
 def read_out(query, intra, gate, back, weight):
     tokens, width = query.shape
     columns = weight.shape[1]
-    pieces = 8
+    pieces = 4
     near = pl.BlockSpec(memory_space=pltpu.VMEM)
     far = pl.BlockSpec(memory_space=pltpu.HBM)
     return pl.pallas_call(

time: 67.9 us -> 67 us (0.987)
  Pallas kernels: 30.8 us -> 29.9 us
    pallas_call x1, Pallas kernels: 5.32 us -> 4.44 us  [read_out(): pl.pallas_call(read_kernel, in_specs=[near, far, far, far, far], out_shap...]
where the time goes in v5:
time: 67 us; the launch traced here: 66.6 us
  Pallas kernels  29.9 us (45%)
  waiting for transfers between devices  21.3 us (32%)
  starting transfers between devices  12.7 us (19%)
  other arithmetic  2.01 us (3%)
  between operations  0.69 us (1%)
    all_to_all x2, waiting for transfers between devices, swap(): return lax.all_to_all(x, 'seq', 0, 0, axis_index_groups=members, tiled=True)  15.3 us
    pallas_call x1, Pallas kernels, local_part(): pl.pallas_call(local_kernel, grid=(heads // step,), in_specs=[narrow, nar...  11.5 us
    all_to_all x2, starting transfers between devices, swap(): return lax.all_to_all(x, 'seq', 0, 0, axis_index_groups=members, tiled=True)  9.95 us
    pallas_call x1, Pallas kernels, group_maps(): pl.pallas_call(lambda *refs: group_kernel(own, keys, *refs), in_specs=[ne...  9.89 us
    ppermute x1, waiting for transfers between devices, local(): lax.ppermute(pair, 'seq', [(i, (i + size) % count) for i in range(count)])  5.61 us
    pallas_call x1, Pallas kernels, read_out(): pl.pallas_call(read_kernel, in_specs=[near, far, far, far, far], out_shap...  4.44 us
    ppermute x1, starting transfers between devices, local(): lax.ppermute(pair, 'seq', [(i, (i + size) % count) for i in range(count)])  2.66 us
    pallas_call x1, Pallas kernels, pack(): pl.pallas_call(pack_kernel, in_specs=[far, far, far, far], out_shape=jax....  2.25 us
  transfers between devices with their start and end apart: 4, of which 4 were waited for; matrix products, arithmetic and copies ran while one was open for 2% of the time, Pallas kernels for 17%

profile of v5, /device:TPU:0, one launch (start us, length us, event | category | flops | bytes accessed | tf_op | source)
XLA Modules:
  0.0 66.6 jit_solution(16589993236757447893)
XLA Ops:
  0.6 2.2 %pack.1 = bf16[8,400,128]{2,1,0:T(8,128)(2,1)} custom-call(bf16[1,128,1024]{2,1,0:T(8,128)(2,1)} %k_ref.3, bf16[1,128,2048]{2,1,0:T(8,128)(2,1)} %v_ref.3, f32[1,16,128]{2,1,0:T(8,128)} %g_ref.3, f32[1,16,128]{2,1,0:T(8,128)} %b_ref.3), custom_call_target="tpu_custom_call" | custom-call | flops 2300000000 | bytes 1048576 | tf_op jit(solution)/shard_map/pack/pallas_call | solution.py:322
  2.9 6.2 %all-to-all-start = ((bf16[8,400,128]{2,1,0:T(8,128)(2,1)}), bf16[8,400,128]{2,1,0:T(8,128)(2,1)S(1)}, u32[]{:S(2)}, u32[]{:S(2)}) async-start(bf16[8,400,128]{2,1,0:T(8,128)(2,1)} %pack.1), calls=%async_computation | async-start | bytes 1638400 | tf_op jit(solution)/shard_map/all_to_all | solution.py:437
  9.1 11.5 %local_part.1 = (bf16[128,2048]{1,0:T(8,128)(2,1)}, f32[128,2048]{1,0:T(8,128)}, f32[128,2048]{1,0:T(8,128)}) custom-call(bf16[1,128,1024]{2,1,0:T(8,128)(2,1)} %q_ref.1, bf16[1,128,1024]{2,1,0:T(8,128)(2,1)} %k_ref.3, bf16[1,128,2048]{2,1,0:T(8,128)(2,1)} %v_ref.3, bf16[1,128,2048]{2,1,0:T(8,128)(2,1)} %z_ref.1, f32[1,16,128]{2,1,0:T(8,128)} %g_ref.3, ...), custom_call_target="tpu_custom_call" | custom-call | flops 13799999488 | bytes 1048576 | tf_op jit(solution)/shard_map/local_part/pallas_call | solution.py:346
  20.6 0.6 all-to-all-done.refs_0_
  21.2 0.0 copy-start.2
  21.2 9.9 %group_maps.1 = (bf16[8,2,128,128]{3,2,1,0:T(8,128)(2,1)S(1)}, f32[8,2,128,128]{3,2,1,0:T(8,128)S(1)}, bf16[2,128,256]{2,1,0:T(8,128)(2,1)S(1)}) custom-call(bf16[8,400,128]{2,1,0:T(8,128)(2,1)S(1)} %all-to-all-done.refs_0_), custom_call_target="tpu_custom_call" | custom-call | flops 13799999488 | bytes 1048576 | tf_op jit(solution)/shard_map/group_maps/pallas_call | solution.py:366
  31.1 0.0 copy-start
  31.1 0.0 copy-start.1
  31.1 2.7 %collective-permute-start = (bf16[2,128,256]{2,1,0:T(8,128)(2,1)S(1)}, bf16[2,128,256]{2,1,0:T(8,128)(2,1)S(1)}, u32[]{:S(2)}, u32[]{:S(2)}) collective-permute-start(bf16[2,128,256]{2,1,0:T(8,128)(2,1)S(1)} %get-tuple-element.18.mine_ref), channel_id=1, source_target_pairs={{0,16},{2,18},{4,20},{6,22},{8,24},{10,26},{12,28},{14,30},{16,0},... | collective-permute-start | bytes 393224 | tf_op jit(solution)/shard_map/ppermute | solution.py:450
  33.7 0.0 copy-done.2
  33.7 0.1 fusion.3
  33.8 0.1 pad_add_fusion.info_ref
  33.9 5.6 %collective-permute-done.got_ref = bf16[2,128,256]{2,1,0:T(8,128)(2,1)S(1)} collective-permute-done((bf16[2,128,256]{2,1,0:T(8,128)(2,1)S(1)}, bf16[2,128,256]{2,1,0:T(8,128)(2,1)S(1)}, u32[]{:S(2)}, u32[]{:S(2)}) %collective-permute-start) | collective-permute-done | bytes 131104 | tf_op jit(solution)/shard_map/ppermute | solution.py:450
  39.5 1.8 %spread_states.1 = bf16[8,2,128,256]{3,2,1,0:T(8,128)(2,1)} custom-call(s32[3]{0:T(128)S(1)} %pad_add_fusion.info_ref, bf16[8,2,128,128]{3,2,1,0:T(8,128)(2,1)S(1)} %get-tuple-element.16.move_ref, f32[8,2,128,128]{3,2,1,0:T(8,128)S(1)} %get-tuple-element.17.add_ref, bf16[2,128,256]{2,1,0:T(8,128)(2,1)S(1)} %get-tuple-element.18.mine_ref, ...), custom_call_target="tpu_custom_call" | custom-call | flops 2300000000 | bytes 1048576 | tf_op jit(solution)/shard_map/spread_states/pallas_call | solution.py:388
  41.3 3.8 %all-to-all-start.1 = ((bf16[8,2,128,256]{3,2,1,0:T(8,128)(2,1)}), bf16[8,2,128,256]{3,2,1,0:T(8,128)(2,1)S(1)}, u32[]{:S(2)}, u32[]{:S(2)}) async-start(bf16[8,2,128,256]{3,2,1,0:T(8,128)(2,1)} %spread_states.1), calls=%async_computation.1 | async-start | bytes 2097152 | tf_op jit(solution)/shard_map/all_to_all | solution.py:437
  45.1 14.7 %all-to-all-done.1 = bf16[8,2,128,256]{3,2,1,0:T(8,128)(2,1)S(1)} async-done(((bf16[8,2,128,256]{3,2,1,0:T(8,128)(2,1)}), bf16[8,2,128,256]{3,2,1,0:T(8,128)(2,1)S(1)}, u32[]{:S(2)}, u32[]{:S(2)}) %all-to-all-start.1) | async-done | bytes 1048608 | tf_op jit(solution)/shard_map/all_to_all | solution.py:437
  59.8 0.0 copy-done
  59.8 0.0 copy-done.1
  59.8 4.4 %read_out.1 = bf16[128,2048]{1,0:T(8,128)(2,1)S(1)} custom-call(bf16[16,128,256]{2,1,0:T(8,128)(2,1)S(1)} %bitcast.12, bf16[128,2048]{1,0:T(8,128)(2,1)S(1)} %copy-done.1, f32[128,2048]{1,0:T(8,128)S(1)} %copy-done, f32[128,2048]{1,0:T(8,128)} %get-tuple-element.21.gate_ref, bf16[2048,2048]{1,0:T(8,128)(2,1)} %w_ref.1), custom_call_target="tpu_custom_call" | custom-call | flops 4600000000 | bytes 1048576 | tf_op jit(solution)/shard_map/read_out/pallas_call | solution.py:404
  64.2 0.1 collective-permute-start.1
  64.3 1.1 %fusion = f32[1,16,128,128]{3,2,1,0:T(8,128)} fusion(bf16[16,128,256]{2,1,0:T(8,128)(2,1)S(1)} %bitcast.13), kind=kLoop, calls=%fused_computation.1 | loop fusion | flops 262144 | bytes 1572864 | tf_op jit(solution)/shard_map/convert_element_type | solution.py:469
  65.4 0.4 collective-permute-done.1
  65.8 0.8 %fusion.1 = bf16[64,1,2048]{2,0,1:T(8,128)(2,1)} fusion(bf16[64,2048]{1,0:T(8,128)(2,1)S(1)} %collective-permute-done.1, bf16[128,2048]{1,0:T(8,128)(2,1)S(1)} %read_out.1, s32[]{:T(128)S(6)} %select_n.24), kind=kLoop, calls=%fused_computation.3 | loop fusion | flops 524288 | bytes 786436 | tf_op jit(solution)/shard_map/broadcast_in_dim | solution.py:481
  (1 shorter events, 0.0 us)
Async XLA Ops:
  2.9 18.3 %all-to-all-start = ((bf16[8,400,128]{2,1,0:T(8,128)(2,1)}), bf16[8,400,128]{2,1,0:T(8,128)(2,1)S(1)}, u32[]{:S(2)}, u32[]{:S(2)}) async-start(bf16[8,400,128]{2,1,0:T(8,128)(2,1)} %pack.1), calls=%async_computation | async-start | bytes 1638400 | tf_op jit(solution)/shard_map/all_to_all | solution.py:437
  21.2 12.6 %copy-start.2 = (s32[1,16]{1,0:T(1,128)S(1)}, s32[1,16]{1,0:T(1,128)}, u32[]{:S(2)}) copy-start(s32[1,16]{1,0:T(1,128)} %param.17) | copy-start | bytes 196
  31.1 28.7 %copy-start = (f32[128,2048]{1,0:T(8,128)S(1)}, f32[128,2048]{1,0:T(8,128)}, u32[]{:S(2)}) copy-start(f32[128,2048]{1,0:T(8,128)} %get-tuple-element.20.intra_ref) | copy-start | bytes 3145732
  31.1 28.7 %copy-start.1 = (bf16[128,2048]{1,0:T(8,128)(2,1)S(1)}, bf16[128,2048]{1,0:T(8,128)(2,1)}, u32[]{:S(2)}) copy-start(bf16[128,2048]{1,0:T(8,128)(2,1)} %get-tuple-element.19.query_ref) | copy-start | bytes 1572868
  31.1 8.4 %collective-permute-start = (bf16[2,128,256]{2,1,0:T(8,128)(2,1)S(1)}, bf16[2,128,256]{2,1,0:T(8,128)(2,1)S(1)}, u32[]{:S(2)}, u32[]{:S(2)}) collective-permute-start(bf16[2,128,256]{2,1,0:T(8,128)(2,1)S(1)} %get-tuple-element.18.mine_ref), channel_id=1, source_target_pairs={{0,16},{2,18},{4,20},{6,22},{8,24},{10,26},{12,28},{14,30},{16,0},... | collective-permute-start | bytes 393224 | tf_op jit(solution)/shard_map/ppermute | solution.py:450
  41.3 18.4 %all-to-all-start.1 = ((bf16[8,2,128,256]{3,2,1,0:T(8,128)(2,1)}), bf16[8,2,128,256]{3,2,1,0:T(8,128)(2,1)S(1)}, u32[]{:S(2)}, u32[]{:S(2)}) async-start(bf16[8,2,128,256]{3,2,1,0:T(8,128)(2,1)} %spread_states.1), calls=%async_computation.1 | async-start | bytes 2097152 | tf_op jit(solution)/shard_map/all_to_all | solution.py:437
  64.2 1.6 %collective-permute-start.1 = (bf16[64,2048]{1,0:T(8,128)(2,1)S(1)}, bf16[64,2048]{1,0:T(8,128)(2,1)S(1)}, u32[]{:S(2)}, u32[]{:S(2)}) collective-permute-start(bf16[64,2048]{1,0:T(8,128)(2,1)S(1)} %constant_dynamic-slice_fusion), channel_id=1, source_target_pairs={{0,1},{1,0},{2,3},{3,2},{4,5},{5,4},{6,7},{7,6},{8,9},{9,8},{10,11... | collective-permute-start | bytes 786440 | tf_op jit(solution)/shard_map/ppermute | solution.py:477
